TPU v7x, 256 devices: a whole 4x4x8 slice. The times are simulated.
256 devices in a mesh: box: 64 (over x, z, core), rhs: 4 (over y).
Axes of the slice: x: 4, y: 4, z: 8, core: 2. Of those that a mesh axis runs over, the one named last changes fastest.
Arguments:
- points: bfloat16 [524288, 64], P('box'), may hold values from -6 to 6
- weights: bfloat16 [524288, 128], P('box', 'rhs'), may hold values from -6 to 6
- near_list: int32 [1024, 12], P('box'), may hold values from 0 to 47, as said below
- near_count: int32 [1024], P('box'), may hold values from 1 to 12, as said below
- skeleton_index: int32 [64, 256], P('box'), may hold values from 0 to 8191, as said below
- skeleton_maps: bfloat16 [64, 256, 8192], P('box'), may hold values from -0.0625 to 0.0625
- level_index: int32 [5, 256], replicated, may hold values from 0 to 511, as said below
- level_maps: bfloat16 [5, 256, 512], replicated, may hold values from -0.25 to 0.25
Outputs:
- product: bfloat16 [524288, 128], P('box', 'rhs')
Inputs may be any that keep to these rules, and one draw needn't show every extreme that they name: `near_list`: entry k of row g is a slot s naming leaf s % 16 of box g // 16 - 1 + s // 16; that box exists, the entries of a row are distinct, and entry 0 names leaf g itself. Only the first near_count[g] entries of row g of near_list are used; some leaf has 12. `skeleton_index`: distinct within a box. `level_index`: distinct within a row.
All inputs are finite; a program needn't handle non-finite values.
Results may differ from a plain program's by a relative error of at most 0.013.
Values may be sent and summed in bfloat16 or wider, within the bound.
No kernel may reach another device: no remote copies, remote signals or barrier semaphores. Data moves between devices by JAX's collectives and lax.ppermute only.
A program may use at most 192 MiB of HBM per device.

v0:
```python
import jax
import jax.numpy as jnp
from jax import lax
from jax.sharding import PartitionSpec as P

LEAF = 512


def from_partner(value, axis, distance):
    mask = 2**distance
    pairs = [(source, source ^ mask) for source in range(lax.axis_size(axis))]
    return lax.ppermute(value, axis, pairs)


def padded(block, sides, width):
    for axis, dim in sides:
        count = lax.axis_size(axis)
        forward = [(i, i + 1) for i in range(count - 1)]
        backward = [(target, source) for source, target in forward]
        low = lax.ppermute(
            lax.slice_in_dim(block, block.shape[dim] - width, None, axis=dim), axis, forward
        )
        high = lax.ppermute(lax.slice_in_dim(block, 0, width, axis=dim), axis, backward)
        block = jnp.concatenate([low, block, high], axis=dim)
    return block


def kernel_apply(rows, centers, values):
    rows_wide = rows.astype(jnp.float32)
    cent_wide = centers.astype(jnp.float32)
    dist = (
        jnp.sum(rows_wide * rows_wide, axis=1)[:, None]
        + jnp.sum(cent_wide * cent_wide, axis=1)[None, :]
    )
    dist = dist - 2.0 * jnp.dot(rows, centers.T, preferred_element_type=jnp.float32)
    kern = jnp.exp(dist * (-2.0 / rows.shape[1])).astype(jnp.bfloat16)
    return jnp.dot(kern, values, preferred_element_type=jnp.float32)


def near_field(points, beside_all, near_list, near_count, first, stride):
    coord_dim = points.shape[1]
    columns = beside_all.shape[1] - coord_dim
    leaf_dev = near_count.shape[0]
    slots_max = near_list.shape[1]
    leaf_blocks = beside_all.reshape(beside_all.shape[0] // LEAF, LEAF, beside_all.shape[1])
    slot_ids = jnp.arange(slots_max, dtype=jnp.int32)

    def leaf_step(leaf, result):
        rows = lax.dynamic_slice_in_dim(points, leaf * LEAF, LEAF, 0)
        slots = near_list[leaf]
        live = (
            (slot_ids < near_count[leaf]) & (slot_ids >= first) & ((slot_ids - first) % stride == 0)
        )
        blocks = jnp.take(leaf_blocks, slots, axis=0)
        centers = blocks[:, :, :coord_dim].reshape(slots_max * LEAF, coord_dim)
        masked = blocks[:, :, coord_dim:] * live.astype(beside_all.dtype)[:, None, None]
        values = masked.reshape(slots_max * LEAF, columns)
        total = kernel_apply(rows, centers, values)
        return lax.dynamic_update_slice_in_dim(result, total, leaf * LEAF, 0)

    return lax.fori_loop(0, leaf_dev, leaf_step, jnp.zeros((points.shape[0], columns), jnp.float32))


def local(
    points, weights, near_list, near_count, skeleton_index, skeleton_maps, level_index, level_maps
):
    coord_dim = points.shape[1]
    width = points.shape[0]
    levels = lax.axis_size("box").bit_length() - 1
    position = lax.axis_index("box")
    own_coords = jnp.take(points, skeleton_index[0], axis=0)
    own_values = jnp.dot(skeleton_maps[0], weights, preferred_element_type=jnp.float32).astype(
        jnp.bfloat16
    )
    own_node = jnp.concatenate([own_coords, own_values], axis=1)
    siblings = []
    for level in range(levels):
        other = from_partner(own_node, "box", level)
        siblings.append(other)
        if level < levels - 1:
            upper_half = jnp.bitwise_and(jnp.right_shift(position, level), 1) == 1
            lower_node = jnp.where(upper_half, other, own_node)
            upper_node = jnp.where(upper_half, own_node, other)
            union = jnp.concatenate([lower_node, upper_node], axis=0)
            picked = jnp.take(union[:, :coord_dim], level_index[level], axis=0)
            merged = jnp.dot(
                level_maps[level], union[:, coord_dim:], preferred_element_type=jnp.float32
            ).astype(jnp.bfloat16)
            own_node = jnp.concatenate([picked, merged], axis=1)
    stacked = jnp.concatenate([points, weights], axis=1)
    beside_all = padded(stacked, (("box", 0),), width)
    near = near_field(points, beside_all, near_list, near_count, 0, 1)
    far = jnp.zeros(near.shape, jnp.float32)
    for level in range(levels):
        other = siblings[level]
        far = far + kernel_apply(points, other[:, :coord_dim], other[:, coord_dim:])
    return (near + far).astype(jnp.bfloat16)


def solution(mesh):
    return jax.shard_map(
        local,
        mesh=mesh,
        in_specs=(
            P("box", None),
            P("box", "rhs"),
            P("box", None),
            P("box"),
            P("box", None),
            P("box", None, None),
            P(),
            P(),
        ),
        out_specs=P("box", "rhs"),
        check_vma=False,
    )
```

profile of v0, /device:TPU:49, one launch (start us, length us, event | category | flops | bytes accessed | tf_op | source)
XLA Modules:
  0.0 333.9 jit_solution(7886260910401168565)
XLA Ops:
  22.4 5.1 %collective-permute-done.3 = bf16[256,96]{1,0:T(8,128)(2,1)S(1)} collective-permute-done((bf16[256,96]{1,0:T(8,128)(2,1)S(1)}, bf16[256,96]{1,0:T(8,128)(2,1)S(1)}, u32[]{:S(2)}, u32[]{:S(2)}) %collective-permute-start.3) | collective-permute-done | bytes 49184 | tf_op jit(solution)/shard_map/ppermute | solution.py:12
  32.6 4.8 %fusion.49 = f32[8192,32]{0,1:T(8,128)} fusion(bf16[8192,64]{0,1:T(8,128)(2,1)} %param.12, f32[256]{0:T(256)S(1)} %multiply_reduce_fusion.7, f32[8192]{0:T(1024)S(1)} %multiply_reduce_fusion.2, bf16[256,96]{1,0:T(8,128)(2,1)S(1)} %collective-permute-done.3), kind=kOutput, calls=%fused_computation.73 | convolution fusion | flops 413138944 | bytes 2262016 | tf_op jit(solution)/shard_map/dot_general | solution.py:37
  39.9 4.9 %collective-permute-start.5 = (bf16[256,96]{1,0:T(8,128)(2,1)S(1)}, bf16[256,96]{1,0:T(8,128)(2,1)S(1)}, u32[]{:S(2)}, u32[]{:S(2)}) collective-permute-start(bf16[256,96]{1,0:T(8,128)(2,1)S(1)} %pad_maximum_fusion.14), channel_id=1, source_target_pairs={{0,32},{4,36},{8,40},{12,44},{16,48},{20,52},{24,56},{28,60},{32,0... | collective-permute-start | bytes 147464 | tf_op jit(solution)/shard_map/ppermute | solution.py:12
  44.9 4.8 %fusion.50 = f32[8192,32]{0,1:T(8,128)} fusion(bf16[8192,64]{0,1:T(8,128)(2,1)} %param.12, f32[256]{0:T(256)S(1)} %multiply_reduce_fusion.6, f32[8192]{0:T(1024)S(1)} %multiply_reduce_fusion.2, bf16[256,96]{1,0:T(8,128)(2,1)S(1)} %collective-permute-done.4), kind=kOutput, calls=%fused_computation.74 | convolution fusion | flops 413138944 | bytes 2262016 | tf_op jit(solution)/shard_map/dot_general | solution.py:37
  53.7 4.8 %fusion.51 = f32[8192,32]{0,1:T(8,128)} fusion(bf16[8192,64]{0,1:T(8,128)(2,1)} %param.12, f32[256]{0:T(256)S(1)} %multiply_reduce_fusion.5, f32[8192]{0:T(1024)S(1)} %multiply_reduce_fusion.2, bf16[256,96]{1,0:T(8,128)(2,1)S(1)} %collective-permute-done.5), kind=kOutput, calls=%fused_computation.75 | convolution fusion | flops 413138944 | bytes 2262016 | tf_op jit(solution)/shard_map/dot_general | solution.py:37
  64.4 4.8 %fusion.52 = f32[8192,32]{0,1:T(8,128)} fusion(bf16[8192,64]{0,1:T(8,128)(2,1)} %param.12, f32[256]{0:T(256)S(1)} %multiply_reduce_fusion.4, f32[8192]{0:T(1024)S(1)} %multiply_reduce_fusion.2, bf16[256,96]{1,0:T(8,128)(2,1)S(1)} %collective-permute-done.6), kind=kOutput, calls=%fused_computation.76 | convolution fusion | flops 413138944 | bytes 2262016 | tf_op jit(solution)/shard_map/dot_general | solution.py:37
  69.3 4.8 %fusion.53 = f32[8192,32]{0,1:T(8,128)} fusion(bf16[8192,64]{0,1:T(8,128)(2,1)} %param.12, f32[256]{0:T(256)S(1)} %multiply_reduce_fusion.3, f32[8192]{0:T(1024)S(1)} %multiply_reduce_fusion.2, bf16[256,96]{1,0:T(8,128)(2,1)S(1)} %collective-permute-done.7), kind=kOutput, calls=%fused_computation.77 | convolution fusion | flops 413138944 | bytes 2262016 | tf_op jit(solution)/shard_map/dot_general | solution.py:37
  74.1 4.0 %pad_maximum_fusion = bf16[24576,96]{0,1:T(8,128)(2,1)} fusion(bf16[8192,96]{0,1:T(8,128)(2,1)} %collective-permute-done.1, bf16[8192,96]{0,1:T(8,128)(2,1)S(1)} %constant_dynamic-update-slice_fusion, bf16[8192,96]{0,1:T(8,128)(2,1)} %collective-permute-done), kind=kLoop, calls=%fused_computation.69 | loop fusion | flops 14155776 | bytes 9437184 | tf_op jit(solution)/shard_map/concatenate | solution.py:24
  78.0 8.0 %copy.17 = bf16[24576,96]{1,0:T(8,128)(2,1)} copy(bf16[24576,96]{0,1:T(8,128)(2,1)} %pad_maximum_fusion) | data formatting | bytes 9437184 | tf_op jit(solution)/shard_map/concatenate | solution.py:24
  87.1 241.0 %while.17 = (s32[]{:T(128)}, f32[8192,32]{0,1:T(8,128)}, bf16[8192,64]{0,1:T(8,128)(2,1)}, s32[16,12]{1,0:T(8,128)}, bf16[48,512,96]{2,1,0:T(8,128)(2,1)}, /*ind...) while((s32[]{:T(128)}, f32[8192,32]{0,1:T(8,128)}, ...), condition=%wide.region_3.4_spmd.clone.clone, body=%wide.region_0.3_spmd.clone.clone.sunk | while | flops 621767296 | bytes 7775727 | solution.py:61
  87.8 3.6 %gather_fusion = bf16[12,512,96]{2,1,0:T(8,128)(2,1)S(1)} fusion(bf16[48,512,96]{2,1,0:T(8,128)(2,1)} %get-tuple-element.312, s32[1024]{0:T(1024)S(1)} %pad_clamp_fusion.8), kind=kCustom, calls=%fused_computation.1.clone.clone.1 | custom fusion | bytes 2359344 | tf_op jit(solution)/shard_map/while/body/eval_jaxpr/jit(_take)/gather | solution.py:54
  96.0 6.1 %fusion.131 = f32[8192,32]{0,1:T(8,128)} fusion(f32[8192,32]{0,1:T(8,128)} %get-tuple-element.299, s32[]{:T(128)S(6)} %select_n.258, bf16[6144,32]{1,0:T(8,128)(2,1)S(1)} %bitcast.150, bf16[6144,64]{1,0:T(8,128)(2,1)S(1)} %bitcast.149, f32[6144]{0:T(1024)S(1)} %add.476, f32[512]{0:T(512)S(1)} %multiply_reduce_fusion.12, ...), kind=kOutput, calls=%fused_computation.13.clone.1 | convolution fusion | flops 619708416 | bytes 1338368 | tf_op jit(solution)/shard_map/while/body/eval_jaxpr/dot_general | solution.py:37
  102.8 3.6 %gather_fusion = bf16[12,512,96]{2,1,0:T(8,128)(2,1)S(1)} fusion(bf16[48,512,96]{2,1,0:T(8,128)(2,1)} %get-tuple-element.312, s32[1024]{0:T(1024)S(1)} %pad_clamp_fusion.8), kind=kCustom, calls=%fused_computation.1.clone.clone.1 | custom fusion | bytes 2359344 | tf_op jit(solution)/shard_map/while/body/eval_jaxpr/jit(_take)/gather | solution.py:54
  111.1 6.1 %fusion.131 = f32[8192,32]{0,1:T(8,128)} fusion(f32[8192,32]{0,1:T(8,128)} %get-tuple-element.299, s32[]{:T(128)S(6)} %select_n.258, bf16[6144,32]{1,0:T(8,128)(2,1)S(1)} %bitcast.150, bf16[6144,64]{1,0:T(8,128)(2,1)S(1)} %bitcast.149, f32[6144]{0:T(1024)S(1)} %add.476, f32[512]{0:T(512)S(1)} %multiply_reduce_fusion.12, ...), kind=kOutput, calls=%fused_computation.13.clone.1 | convolution fusion | flops 619708416 | bytes 1338368 | tf_op jit(solution)/shard_map/while/body/eval_jaxpr/dot_general | solution.py:37
  117.9 3.6 %gather_fusion = bf16[12,512,96]{2,1,0:T(8,128)(2,1)S(1)} fusion(bf16[48,512,96]{2,1,0:T(8,128)(2,1)} %get-tuple-element.312, s32[1024]{0:T(1024)S(1)} %pad_clamp_fusion.8), kind=kCustom, calls=%fused_computation.1.clone.clone.1 | custom fusion | bytes 2359344 | tf_op jit(solution)/shard_map/while/body/eval_jaxpr/jit(_take)/gather | solution.py:54
  126.1 6.1 %fusion.131 = f32[8192,32]{0,1:T(8,128)} fusion(f32[8192,32]{0,1:T(8,128)} %get-tuple-element.299, s32[]{:T(128)S(6)} %select_n.258, bf16[6144,32]{1,0:T(8,128)(2,1)S(1)} %bitcast.150, bf16[6144,64]{1,0:T(8,128)(2,1)S(1)} %bitcast.149, f32[6144]{0:T(1024)S(1)} %add.476, f32[512]{0:T(512)S(1)} %multiply_reduce_fusion.12, ...), kind=kOutput, calls=%fused_computation.13.clone.1 | convolution fusion | flops 619708416 | bytes 1338368 | tf_op jit(solution)/shard_map/while/body/eval_jaxpr/dot_general | solution.py:37
  141.2 6.1 %fusion.131 = f32[8192,32]{0,1:T(8,128)} fusion(f32[8192,32]{0,1:T(8,128)} %get-tuple-element.299, s32[]{:T(128)S(6)} %select_n.258, bf16[6144,32]{1,0:T(8,128)(2,1)S(1)} %bitcast.150, bf16[6144,64]{1,0:T(8,128)(2,1)S(1)} %bitcast.149, f32[6144]{0:T(1024)S(1)} %add.476, f32[512]{0:T(512)S(1)} %multiply_reduce_fusion.12, ...), kind=kOutput, calls=%fused_computation.13.clone.1 | convolution fusion | flops 619708416 | bytes 1338368 | tf_op jit(solution)/shard_map/while/body/eval_jaxpr/dot_general | solution.py:37
  156.2 6.1 %fusion.131 = f32[8192,32]{0,1:T(8,128)} fusion(f32[8192,32]{0,1:T(8,128)} %get-tuple-element.299, s32[]{:T(128)S(6)} %select_n.258, bf16[6144,32]{1,0:T(8,128)(2,1)S(1)} %bitcast.150, bf16[6144,64]{1,0:T(8,128)(2,1)S(1)} %bitcast.149, f32[6144]{0:T(1024)S(1)} %add.476, f32[512]{0:T(512)S(1)} %multiply_reduce_fusion.12, ...), kind=kOutput, calls=%fused_computation.13.clone.1 | convolution fusion | flops 619708416 | bytes 1338368 | tf_op jit(solution)/shard_map/while/body/eval_jaxpr/dot_general | solution.py:37
  171.3 6.1 %fusion.131 = f32[8192,32]{0,1:T(8,128)} fusion(f32[8192,32]{0,1:T(8,128)} %get-tuple-element.299, s32[]{:T(128)S(6)} %select_n.258, bf16[6144,32]{1,0:T(8,128)(2,1)S(1)} %bitcast.150, bf16[6144,64]{1,0:T(8,128)(2,1)S(1)} %bitcast.149, f32[6144]{0:T(1024)S(1)} %add.476, f32[512]{0:T(512)S(1)} %multiply_reduce_fusion.12, ...), kind=kOutput, calls=%fused_computation.13.clone.1 | convolution fusion | flops 619708416 | bytes 1338368 | tf_op jit(solution)/shard_map/while/body/eval_jaxpr/dot_general | solution.py:37
  178.1 3.6 %gather_fusion = bf16[12,512,96]{2,1,0:T(8,128)(2,1)S(1)} fusion(bf16[48,512,96]{2,1,0:T(8,128)(2,1)} %get-tuple-element.312, s32[1024]{0:T(1024)S(1)} %pad_clamp_fusion.8), kind=kCustom, calls=%fused_computation.1.clone.clone.1 | custom fusion | bytes 2359344 | tf_op jit(solution)/shard_map/while/body/eval_jaxpr/jit(_take)/gather | solution.py:54
  186.4 6.1 %fusion.131 = f32[8192,32]{0,1:T(8,128)} fusion(f32[8192,32]{0,1:T(8,128)} %get-tuple-element.299, s32[]{:T(128)S(6)} %select_n.258, bf16[6144,32]{1,0:T(8,128)(2,1)S(1)} %bitcast.150, bf16[6144,64]{1,0:T(8,128)(2,1)S(1)} %bitcast.149, f32[6144]{0:T(1024)S(1)} %add.476, f32[512]{0:T(512)S(1)} %multiply_reduce_fusion.12, ...), kind=kOutput, calls=%fused_computation.13.clone.1 | convolution fusion | flops 619708416 | bytes 1338368 | tf_op jit(solution)/shard_map/while/body/eval_jaxpr/dot_general | solution.py:37
  201.4 6.1 %fusion.131 = f32[8192,32]{0,1:T(8,128)} fusion(f32[8192,32]{0,1:T(8,128)} %get-tuple-element.299, s32[]{:T(128)S(6)} %select_n.258, bf16[6144,32]{1,0:T(8,128)(2,1)S(1)} %bitcast.150, bf16[6144,64]{1,0:T(8,128)(2,1)S(1)} %bitcast.149, f32[6144]{0:T(1024)S(1)} %add.476, f32[512]{0:T(512)S(1)} %multiply_reduce_fusion.12, ...), kind=kOutput, calls=%fused_computation.13.clone.1 | convolution fusion | flops 619708416 | bytes 1338368 | tf_op jit(solution)/shard_map/while/body/eval_jaxpr/dot_general | solution.py:37
  216.5 6.1 %fusion.131 = f32[8192,32]{0,1:T(8,128)} fusion(f32[8192,32]{0,1:T(8,128)} %get-tuple-element.299, s32[]{:T(128)S(6)} %select_n.258, bf16[6144,32]{1,0:T(8,128)(2,1)S(1)} %bitcast.150, bf16[6144,64]{1,0:T(8,128)(2,1)S(1)} %bitcast.149, f32[6144]{0:T(1024)S(1)} %add.476, f32[512]{0:T(512)S(1)} %multiply_reduce_fusion.12, ...), kind=kOutput, calls=%fused_computation.13.clone.1 | convolution fusion | flops 619708416 | bytes 1338368 | tf_op jit(solution)/shard_map/while/body/eval_jaxpr/dot_general | solution.py:37
  231.6 6.1 %fusion.131 = f32[8192,32]{0,1:T(8,128)} fusion(f32[8192,32]{0,1:T(8,128)} %get-tuple-element.299, s32[]{:T(128)S(6)} %select_n.258, bf16[6144,32]{1,0:T(8,128)(2,1)S(1)} %bitcast.150, bf16[6144,64]{1,0:T(8,128)(2,1)S(1)} %bitcast.149, f32[6144]{0:T(1024)S(1)} %add.476, f32[512]{0:T(512)S(1)} %multiply_reduce_fusion.12, ...), kind=kOutput, calls=%fused_computation.13.clone.1 | convolution fusion | flops 619708416 | bytes 1338368 | tf_op jit(solution)/shard_map/while/body/eval_jaxpr/dot_general | solution.py:37
  246.6 6.1 %fusion.131 = f32[8192,32]{0,1:T(8,128)} fusion(f32[8192,32]{0,1:T(8,128)} %get-tuple-element.299, s32[]{:T(128)S(6)} %select_n.258, bf16[6144,32]{1,0:T(8,128)(2,1)S(1)} %bitcast.150, bf16[6144,64]{1,0:T(8,128)(2,1)S(1)} %bitcast.149, f32[6144]{0:T(1024)S(1)} %add.476, f32[512]{0:T(512)S(1)} %multiply_reduce_fusion.12, ...), kind=kOutput, calls=%fused_computation.13.clone.1 | convolution fusion | flops 619708416 | bytes 1338368 | tf_op jit(solution)/shard_map/while/body/eval_jaxpr/dot_general | solution.py:37
  261.7 6.1 %fusion.131 = f32[8192,32]{0,1:T(8,128)} fusion(f32[8192,32]{0,1:T(8,128)} %get-tuple-element.299, s32[]{:T(128)S(6)} %select_n.258, bf16[6144,32]{1,0:T(8,128)(2,1)S(1)} %bitcast.150, bf16[6144,64]{1,0:T(8,128)(2,1)S(1)} %bitcast.149, f32[6144]{0:T(1024)S(1)} %add.476, f32[512]{0:T(512)S(1)} %multiply_reduce_fusion.12, ...), kind=kOutput, calls=%fused_computation.13.clone.1 | convolution fusion | flops 619708416 | bytes 1338368 | tf_op jit(solution)/shard_map/while/body/eval_jaxpr/dot_general | solution.py:37
  276.8 6.1 %fusion.131 = f32[8192,32]{0,1:T(8,128)} fusion(f32[8192,32]{0,1:T(8,128)} %get-tuple-element.299, s32[]{:T(128)S(6)} %select_n.258, bf16[6144,32]{1,0:T(8,128)(2,1)S(1)} %bitcast.150, bf16[6144,64]{1,0:T(8,128)(2,1)S(1)} %bitcast.149, f32[6144]{0:T(1024)S(1)} %add.476, f32[512]{0:T(512)S(1)} %multiply_reduce_fusion.12, ...), kind=kOutput, calls=%fused_computation.13.clone.1 | convolution fusion | flops 619708416 | bytes 1338368 | tf_op jit(solution)/shard_map/while/body/eval_jaxpr/dot_general | solution.py:37
  283.6 3.6 %gather_fusion = bf16[12,512,96]{2,1,0:T(8,128)(2,1)S(1)} fusion(bf16[48,512,96]{2,1,0:T(8,128)(2,1)} %get-tuple-element.312, s32[1024]{0:T(1024)S(1)} %pad_clamp_fusion.8), kind=kCustom, calls=%fused_computation.1.clone.clone.1 | custom fusion | bytes 2359344 | tf_op jit(solution)/shard_map/while/body/eval_jaxpr/jit(_take)/gather | solution.py:54
  291.8 6.1 %fusion.131 = f32[8192,32]{0,1:T(8,128)} fusion(f32[8192,32]{0,1:T(8,128)} %get-tuple-element.299, s32[]{:T(128)S(6)} %select_n.258, bf16[6144,32]{1,0:T(8,128)(2,1)S(1)} %bitcast.150, bf16[6144,64]{1,0:T(8,128)(2,1)S(1)} %bitcast.149, f32[6144]{0:T(1024)S(1)} %add.476, f32[512]{0:T(512)S(1)} %multiply_reduce_fusion.12, ...), kind=kOutput, calls=%fused_computation.13.clone.1 | convolution fusion | flops 619708416 | bytes 1338368 | tf_op jit(solution)/shard_map/while/body/eval_jaxpr/dot_general | solution.py:37
  306.9 6.1 %fusion.131 = f32[8192,32]{0,1:T(8,128)} fusion(f32[8192,32]{0,1:T(8,128)} %get-tuple-element.299, s32[]{:T(128)S(6)} %select_n.258, bf16[6144,32]{1,0:T(8,128)(2,1)S(1)} %bitcast.150, bf16[6144,64]{1,0:T(8,128)(2,1)S(1)} %bitcast.149, f32[6144]{0:T(1024)S(1)} %add.476, f32[512]{0:T(512)S(1)} %multiply_reduce_fusion.12, ...), kind=kOutput, calls=%fused_computation.13.clone.1 | convolution fusion | flops 619708416 | bytes 1338368 | tf_op jit(solution)/shard_map/while/body/eval_jaxpr/dot_general | solution.py:37
  321.9 6.1 %fusion.131 = f32[8192,32]{0,1:T(8,128)} fusion(f32[8192,32]{0,1:T(8,128)} %get-tuple-element.299, s32[]{:T(128)S(6)} %select_n.258, bf16[6144,32]{1,0:T(8,128)(2,1)S(1)} %bitcast.150, bf16[6144,64]{1,0:T(8,128)(2,1)S(1)} %bitcast.149, f32[6144]{0:T(1024)S(1)} %add.476, f32[512]{0:T(512)S(1)} %multiply_reduce_fusion.12, ...), kind=kOutput, calls=%fused_computation.13.clone.1 | convolution fusion | flops 619708416 | bytes 1338368 | tf_op jit(solution)/shard_map/while/body/eval_jaxpr/dot_general | solution.py:37
  328.1 5.8 %fusion.46 = bf16[8192,32]{0,1:T(8,128)(2,1)} fusion(f32[8192,32]{0,1:T(8,128)} %get-tuple-element.185, f32[8192,32]{0,1:T(8,128)} %fusion.53, f32[8192,32]{0,1:T(8,128)} %fusion.52, f32[8192,32]{0,1:T(8,128)} %fusion.51, f32[8192,32]{0,1:T(8,128)} %fusion.50, f32[8192,32]{0,1:T(8,128)} %fusion.49, bf16[8192,64]{0,1:T(8,128)(2,1)} %param.12, ...), kind=kOutput, calls=%fused_computation.68 | convolution fusion | flops 414973952 | bytes 8029184 | tf_op jit(solution)/shard_map/dot_general | solution.py:37
  (260 shorter events, 165.0 us)
Async XLA Ops:
  0.0 11.3 %copy-start = (bf16[8192,32]{0,1:T(8,128)(2,1)S(1)}, bf16[8192,32]{0,1:T(8,128)(2,1)}, u32[]{:S(2)}) copy-start(bf16[8192,32]{0,1:T(8,128)(2,1)} %param.13) | copy-start | bytes 1572868
  0.0 14.9 %copy-start.1 = (s32[5,256]{1,0:T(8,128)S(1)}, s32[5,256]{1,0:T(8,128)}, u32[]{:S(2)}) copy-start(s32[5,256]{1,0:T(8,128)} %param.18) | copy-start | bytes 15364
  0.0 15.0 %copy-start.2 = (s32[1,256]{1,0:T(1,128)S(1)}, s32[1,256]{1,0:T(1,128)}, u32[]{:S(2)}) copy-start(s32[1,256]{1,0:T(1,128)} %param.16) | copy-start | bytes 3076
  2.4 71.6 %collective-permute-start.1 = (bf16[8192,96]{0,1:T(8,128)(2,1)S(1)}, bf16[8192,96]{0,1:T(8,128)(2,1)}, u32[]{:S(2)}, u32[]{:S(2)}) collective-permute-start(bf16[8192,96]{0,1:T(8,128)(2,1)S(1)} %constant_dynamic-update-slice_fusion), channel_id=1, source_target_pairs={{4,0},{8,4},{12,8},{16,12},{20,16},{24,20},{28,24},{32,28},{36,32}... | collective-permute-start | bytes 4718600 | tf_op jit(solution)/shard_map/ppermute | solution.py:23
  5.0 69.0 %collective-permute-start = (bf16[8192,96]{0,1:T(8,128)(2,1)S(1)}, bf16[8192,96]{0,1:T(8,128)(2,1)}, u32[]{:S(2)}, u32[]{:S(2)}) collective-permute-start(bf16[8192,96]{0,1:T(8,128)(2,1)S(1)} %constant_dynamic-update-slice_fusion), channel_id=1, source_target_pairs={{0,4},{4,8},{8,12},{12,16},{16,20},{20,24},{24,28},{28,32},{32,36}... | collective-permute-start | bytes 4718600 | tf_op jit(solution)/shard_map/ppermute | solution.py:20
  17.8 1.8 collective-permute-start.2
  22.2 5.3 %collective-permute-start.3 = (bf16[256,96]{1,0:T(8,128)(2,1)S(1)}, bf16[256,96]{1,0:T(8,128)(2,1)S(1)}, u32[]{:S(2)}, u32[]{:S(2)}) collective-permute-start(bf16[256,96]{1,0:T(8,128)(2,1)S(1)} %pad_maximum_fusion.12), channel_id=1, source_target_pairs={{0,8},{4,12},{8,0},{12,4},{16,24},{20,28},{24,16},{28,20},{32,40},... | collective-permute-start | bytes 147464 | tf_op jit(solution)/shard_map/ppermute | solution.py:12
  30.1 7.3 %collective-permute-start.4 = (bf16[256,96]{1,0:T(8,128)(2,1)S(1)}, bf16[256,96]{1,0:T(8,128)(2,1)S(1)}, u32[]{:S(2)}, u32[]{:S(2)}) collective-permute-start(bf16[256,96]{1,0:T(8,128)(2,1)S(1)} %pad_maximum_fusion.13), channel_id=1, source_target_pairs={{0,16},{4,20},{8,24},{12,28},{16,0},{20,4},{24,8},{28,12},{32,48},... | collective-permute-start | bytes 147464 | tf_op jit(solution)/shard_map/ppermute | solution.py:12
  39.9 9.8 %collective-permute-start.5 = (bf16[256,96]{1,0:T(8,128)(2,1)S(1)}, bf16[256,96]{1,0:T(8,128)(2,1)S(1)}, u32[]{:S(2)}, u32[]{:S(2)}) collective-permute-start(bf16[256,96]{1,0:T(8,128)(2,1)S(1)} %pad_maximum_fusion.14), channel_id=1, source_target_pairs={{0,32},{4,36},{8,40},{12,44},{16,48},{20,52},{24,56},{28,60},{32,0... | collective-permute-start | bytes 147464 | tf_op jit(solution)/shard_map/ppermute | solution.py:12
  52.3 6.2 %collective-permute-start.6 = (bf16[256,96]{1,0:T(8,128)(2,1)S(1)}, bf16[256,96]{1,0:T(8,128)(2,1)S(1)}, u32[]{:S(2)}, u32[]{:S(2)}) collective-permute-start(bf16[256,96]{1,0:T(8,128)(2,1)S(1)} %pad_maximum_fusion.15), channel_id=1, source_target_pairs={{0,64},{4,68},{8,72},{12,76},{16,80},{20,84},{24,88},{28,92},{32,9... | collective-permute-start | bytes 147464 | tf_op jit(solution)/shard_map/ppermute | solution.py:12
  61.0 8.1 %collective-permute-start.7 = (bf16[256,96]{1,0:T(8,128)(2,1)S(1)}, bf16[256,96]{1,0:T(8,128)(2,1)S(1)}, u32[]{:S(2)}, u32[]{:S(2)}) collective-permute-start(bf16[256,96]{1,0:T(8,128)(2,1)S(1)} %pad_maximum_fusion.16), channel_id=1, source_target_pairs={{0,128},{4,132},{8,136},{12,140},{16,144},{20,148},{24,152},{28,15... | collective-permute-start | bytes 147464 | tf_op jit(solution)/shard_map/ppermute | solution.py:12
  78.0 9.1 %copy-start.3 = (s32[16]{0:T(128)S(1)}, s32[16]{0:T(128)}, u32[]{:S(2)}) copy-start(s32[16]{0:T(128)} %param.15) | copy-start | bytes 196
where the time goes:
time: 339 us; the launch traced here: 334 us
  matrix products  137 us (40%)
  local copies, waits for them, and re-layouts  90.8 us (27%)
  other arithmetic  81.5 us (24%)
  starting transfers between devices  18 us (5%)
  waiting for transfers between devices  5.15 us (2%)
    dot_general x22, matrix products, kernel_apply(): return jnp.dot(kern, values, preferred_element_type=jnp.float32)  128 us
    gather x16, local copies, waits for them, and re-layouts, leaf_step(): blocks = jnp.take(leaf_blocks, slots, axis=0)  58.1 us
    reduce_sum x17, other arithmetic, kernel_apply(): jnp.sum(rows_wide * rows_wide, axis=1)[:, None]  15.5 us
    reduce_sum x22, other arithmetic, kernel_apply(): jnp.sum(cent_wide * cent_wide, axis=1)[None, :]  14.8 us
    select_n x32, other arithmetic, leaf_step(): blocks = jnp.take(leaf_blocks, slots, axis=0)  14.5 us
    ppermute x6, starting transfers between devices, from_partner(): return lax.ppermute(value, axis, pairs)  12 us
    and x16, other arithmetic, leaf_step(): blocks = jnp.take(leaf_blocks, slots, axis=0)  11.3 us
    convert_element_type x16, other arithmetic, leaf_step(): live.astype(beside_all.dtype)[:, None, None]  11 us
  transfers between devices with their start and end apart: 8, of which 1 were waited for; matrix products, arithmetic and copies ran while one was open for 14% of the time, Pallas kernels for 0%

commit v1 on v0

v1 whole, which is shorter than its diff:
```python
import functools

import jax
import jax.numpy as jnp
from jax import lax
from jax.experimental import pallas as pl
from jax.experimental.pallas import tpu as pltpu
from jax.sharding import PartitionSpec as P

LEAF = 512
HALF = 256
UNROLL = 16
AHEAD = 2
LIST = 512
DEPTH = 128
ROW_BITS = 5
VMEM = 40 * 2**20
F32 = jnp.float32
BF16 = jnp.bfloat16
NT = (((1,), (1,)), ((), ()))
TN = (((0,), (0,)), ((), ()))


def in_vmem():
    return pl.BlockSpec(memory_space=pltpu.VMEM)


def in_smem():
    return pl.BlockSpec(memory_space=pltpu.SMEM)


def params():
    return pltpu.CompilerParams(vmem_limit_bytes=VMEM)


def write_lists(near_list, near_count, lists, counts, far_blocks):
    leaves, slots = near_list.shape
    first_far = 2 * leaves
    for seg in range(3):
        counts[seg] = 0

    def leaf_body(leaf, _):
        def slot_body(k, _):
            slot = near_list[leaf, k]
            seg = slot // leaves
            at = counts[seg]
            item = ((slot - seg * leaves) * 2) * 2**ROW_BITS + leaf
            lists[seg, at] = item
            lists[seg, at + 1] = item + 2**ROW_BITS
            counts[seg] = at + 2
            return 0

        return lax.fori_loop(0, near_count[leaf], slot_body, 0)

    lax.fori_loop(0, leaves, leaf_body, 0)
    for seg in range(3):

        def far_body(leaf, at, seg=seg):
            for block in range(far_blocks[seg]):
                lists[seg, at + block] = (first_far + block) * 2**ROW_BITS + leaf
            return at + far_blocks[seg]

        end = lax.fori_loop(0, leaves, far_body, counts[seg])
        counts[seg] = end
        for pad in range(UNROLL):
            lists[seg, end + pad] = leaves


def skeleton_kernel(chunk, far_blocks, near_list, near_count, index, points, weights, maps, node, lists, counts, coords, values):
    step = pl.program_id(0)

    @pl.when(step == 0)
    def _():
        coords[...] = jnp.zeros_like(coords)
        values[...] = jnp.zeros_like(values)
        write_lists(near_list, near_count, lists, counts, far_blocks)

    rows = lax.broadcasted_iota(jnp.int32, (chunk, index.shape[1]), 0) + step * chunk
    pick = jnp.where(rows == index[...], 1.0, 0.0).astype(BF16)
    coords[...] += jnp.dot(points[...], pick, preferred_element_type=F32)
    values[...] += lax.dot_general(weights[...], maps[0], NT, preferred_element_type=F32)

    @pl.when(step == pl.num_programs(0) - 1)
    def _():
        dim = coords.shape[0]
        node[:dim, :] = coords[...].astype(BF16)
        node[dim:, :] = values[...].astype(BF16)


def skeleton(points, weights, near_list, near_count, index, maps, far_blocks):
    dim, width = points.shape
    columns = weights.shape[0]
    size = index.shape[1]
    chunk = 1024
    return pl.pallas_call(
        functools.partial(skeleton_kernel, chunk, far_blocks),
        grid=(width // chunk,),
        out_shape=(
            jax.ShapeDtypeStruct((dim + columns, size), BF16),
            jax.ShapeDtypeStruct((3, LIST), jnp.int32),
            jax.ShapeDtypeStruct((3,), jnp.int32),
        ),
        in_specs=[
            in_smem(),
            in_smem(),
            pl.BlockSpec((1, size), lambda i: (0, 0)),
            pl.BlockSpec((dim, chunk), lambda i: (0, i)),
            pl.BlockSpec((columns, chunk), lambda i: (0, i)),
            pl.BlockSpec((1, size, chunk), lambda i: (0, 0, i)),
        ],
        out_specs=(pl.BlockSpec((dim + columns, size), lambda i: (0, 0)), in_smem(), in_smem()),
        scratch_shapes=[pltpu.VMEM((dim, size), F32), pltpu.VMEM((columns, size), F32)],
        compiler_params=params(),
        name="skeleton",
    )(near_list, near_count, index, points, weights, maps)


def merge(dim, lower, upper, index, level_map):
    union = jnp.concatenate([lower, upper], axis=1)
    rows = lax.broadcasted_iota(jnp.int32, (union.shape[1], index.shape[1]), 0)
    pick = jnp.where(rows == index, 1.0, 0.0).astype(BF16)
    picked = jnp.dot(union[:dim], pick, preferred_element_type=F32)
    merged = lax.dot_general(union[dim:], level_map, NT, preferred_element_type=F32)
    return jnp.concatenate([picked, merged], axis=0).astype(BF16)


def climb_kernel(dim, level, last, position, index, maps, own, one, two, three, sibling, parent=None):
    low_bit = jnp.bitwise_and(position[0], 1)
    high_bit = jnp.bitwise_and(position[0] // 2, 1)

    def ordered(bit, same, other):
        is_upper = bit == 1
        same, other = same.astype(F32), other.astype(F32)
        lower = jnp.where(is_upper, other, same).astype(BF16)
        return lower, jnp.where(is_upper, same, other).astype(BF16)

    index_here = index[level : level + 1, :]
    lower, upper = ordered(low_bit, two[...], three[...])
    aside = merge(dim, lower, upper, index_here, maps[level])
    sibling[...] = aside
    if not last:
        lower, upper = ordered(low_bit, own[...], one[...])
        mine = merge(dim, lower, upper, index_here, maps[level])
        lower, upper = ordered(high_bit, mine, aside)
        parent[...] = merge(dim, lower, upper, index[level + 1 : level + 2, :], maps[level + 1])


def climb(dim, level, last, position, index, maps, nodes):
    shape = jax.ShapeDtypeStruct(nodes[0].shape, BF16)
    return pl.pallas_call(
        functools.partial(climb_kernel, dim, level, last),
        out_shape=(shape,) if last else (shape, shape),
        in_specs=[in_smem()] + [in_vmem()] * 6,
        out_specs=(in_vmem(),) if last else (in_vmem(), in_vmem()),
        compiler_params=params(),
        name="climb",
    )(jnp.reshape(position, (1,)).astype(jnp.int32), index, maps, *nodes)


def three_partners(node, level):
    nodes = [node]
    for mask in (1, 2, 3):
        pairs = [(i, i ^ (mask << level)) for i in range(lax.axis_size("box"))]
        nodes.append(lax.ppermute(node, "box", pairs))
    return nodes


def add_norm_rows(target, source, negative, at, width):
    dim = source.shape[0]
    piece = min(LEAF, width)
    target[dim + 16 :, at : at + width] = jnp.zeros((DEPTH - dim - 16, width), BF16)
    scale = 2.0 / dim

    def body(i, _):
        here = pl.ds(pl.multiple_of(i * piece, piece), piece)
        there = pl.ds(pl.multiple_of(at + i * piece, piece), piece)
        wide = source[:, here].astype(F32)
        norm = jnp.sum(wide * wide, axis=0, keepdims=True) * scale
        high = norm.astype(BF16).astype(F32)
        middle = (norm - high).astype(BF16).astype(F32)
        low = norm - high - middle
        row = lax.broadcasted_iota(jnp.int32, (16, piece), 0)
        first = 3 if negative else 0
        sign = -1.0 if negative else 1.0
        rows = jnp.where(row == first, high, jnp.where(row == first + 1, middle, low))
        norm_rows = (row >= first) & (row < first + 3)
        rows = jnp.where(norm_rows, rows, jnp.where(row < 6, 1.0, 0.0)) * sign
        target[:dim, there] = (wide * (2.0 * scale) ** 0.5).astype(BF16)
        target[dim : dim + 16, there] = rows.astype(BF16)
        return 0

    lax.fori_loop(0, width // piece, body, 0)


def pair_kernel(seg, n_nodes, has_box, has_start, final, *refs):
    refs = list(refs)
    lists, counts, own = refs[:3]
    del refs[:3]
    box = refs[:2] if has_box else []
    del refs[: len(box)]
    nodes = refs[:n_nodes]
    del refs[:n_nodes]
    start = refs.pop(0) if has_start else None
    out, rows, centers, values, total = refs
    dim, width = own.shape
    leaves = width // LEAF
    columns = values.shape[0]

    add_norm_rows(rows, own, False, 0, width)
    rows[:, width:] = jnp.zeros((DEPTH, LEAF), BF16)
    at = 0
    if has_box:
        add_norm_rows(centers, box[0], True, 0, width)
        values[:, :width] = box[1][...]
        at = width
    for node in nodes:
        add_norm_rows(centers, node.at[:dim], True, at, HALF)
        values[:, at : at + HALF] = node[dim:, :]
        at += HALF
    total[:, width:] = jnp.zeros((columns, LEAF), F32)
    total[:, :width] = start[...] if has_start else jnp.zeros((columns, width), F32)

    def run(items):
        items = [
            (pl.ds(pl.multiple_of(source * HALF, HALF), HALF), pl.ds(pl.multiple_of(leaf * LEAF, LEAF), LEAF))
            for source, leaf in items
        ]

        def exponents(item):
            return lax.dot_general(centers[:, item[0]], rows[:, item[1]], TN, preferred_element_type=F32)

        ahead = [exponents(item) for item in items[:AHEAD]]
        for n, item in enumerate(items):
            kern = jnp.exp(ahead[n]).astype(BF16)
            if n + AHEAD < len(items):
                ahead.append(exponents(items[n + AHEAD]))
            total[:, item[1]] += jnp.dot(values[:, item[0]], kern, preferred_element_type=F32)

    if has_box:

        def body(i, _):
            items = []
            for n in range(UNROLL):
                item = lists[seg, i * UNROLL + n]
                items.append((jnp.right_shift(item, ROW_BITS), jnp.bitwise_and(item, 2**ROW_BITS - 1)))
            run(items)
            return 0

        lax.fori_loop(0, (counts[seg] + UNROLL - 1) // UNROLL, body, 0)
    else:
        each = UNROLL // n_nodes

        def body(i, _):
            run([(node, i * each + n) for n in range(each) for node in range(n_nodes)])
            return 0

        lax.fori_loop(0, leaves // each, body, 0)
    out[...] = total[:, :width].astype(out.dtype)


def pairs(seg, lists, counts, own, box, nodes, start, final):
    dim, width = own.shape
    columns = nodes[0].shape[0] - dim if nodes else box[1].shape[0]
    sources = (width if box else 0) + HALF * len(nodes)
    args = [lists, counts, own, *box, *nodes] + ([] if start is None else [start])
    return pl.pallas_call(
        functools.partial(pair_kernel, seg, len(nodes), bool(box), start is not None, final),
        out_shape=jax.ShapeDtypeStruct((columns, width), BF16 if final else F32),
        in_specs=[in_smem(), in_smem()] + [in_vmem()] * (len(args) - 2),
        out_specs=in_vmem(),
        scratch_shapes=[
            pltpu.VMEM((DEPTH, width + LEAF), BF16),
            pltpu.VMEM((DEPTH, sources), BF16),
            pltpu.VMEM((columns, sources), BF16),
            pltpu.VMEM((columns, width + LEAF), F32),
        ],
        compiler_params=params(),
        name="pairs",
    )(*args)


def local(points, weights, near_list, near_count, skeleton_index, skeleton_maps, level_index, level_maps):
    points, weights = points.T, weights.T
    dim = points.shape[0]
    count = lax.axis_size("box")
    position = lax.axis_index("box")
    up = [(i, i + 1) for i in range(count - 1)]
    down = [(i + 1, i) for i in range(count - 1)]
    before = [lax.ppermute(a, "box", up) for a in (points, weights)]
    after = [lax.ppermute(a, "box", down) for a in (points, weights)]
    node, lists, counts = skeleton(
        points, weights, near_list, near_count, skeleton_index, skeleton_maps, (2, 0, 2)
    )
    nodes = three_partners(node, 0)
    total = pairs(1, lists, counts, points, (points, weights), [], None, False)
    sibling_1, node = climb(dim, 0, False, position, level_index, level_maps, nodes)
    siblings = [nodes[1], sibling_1]
    nodes = three_partners(node, 2)
    total = pairs(0, lists, counts, points, before, siblings, total, False)
    sibling_3, node = climb(dim, 2, False, position // 4, level_index, level_maps, nodes)
    siblings = [nodes[1], sibling_3]
    nodes = three_partners(node, 4)
    total = pairs(2, lists, counts, points, after, siblings, total, False)
    (sibling_5,) = climb(dim, 4, True, position // 16, level_index, level_maps, nodes)
    total = pairs(0, lists, counts, points, (), [nodes[1], sibling_5], total, True)
    return total.T


def solution(mesh):
    return jax.shard_map(
        local,
        mesh=mesh,
        in_specs=(
            P("box", None),
            P("box", "rhs"),
            P("box", None),
            P("box"),
            P("box", None),
            P("box", None, None),
            P(),
            P(),
        ),
        out_specs=P("box", "rhs"),
        check_vma=False,
    )
```

time: 339 us -> 131 us (0.39)
  matrix products: 137 us -> 0 us
  other arithmetic: 81.5 us -> 0 us
  local copies, waits for them, and re-layouts: 90.8 us -> 14.9 us
  Pallas kernels: 0 us -> 62.8 us
  starting transfers between devices: 18 us -> 36.5 us
  waiting for transfers between devices: 5.15 us -> 14.5 us
    dot_general x28 -> x0, matrix products: 137 us -> none  [the longest x22 128 us: kernel_apply(): return jnp.dot(kern, values, preferred_element_type=jnp.float32)]
    gather x22 -> x0, local copies, waits for them, and re-layouts: 65 us -> none  [the longest x16 58.1 us: leaf_step(): blocks = jnp.take(leaf_blocks, slots, axis=0)]
    pallas_call x0 -> x8, Pallas kernels: none -> 62.8 us  [the longest x4 51.6 us: pairs(): pl.pallas_call(functools.partial(pair_kernel, seg, len(nodes), bool(box),...]
    reduce_sum x39 -> x0, other arithmetic: 30.3 us -> none  [the longest x17 15.5 us: kernel_apply(): jnp.sum(rows_wide * rows_wide, axis=1)[:, None]]
    ppermute x8 -> x13, starting transfers between devices: 18 us -> 36.5 us  [the longest x9 24.9 us: three_partners(): nodes.append(lax.ppermute(node, 'box', pairs))]
    select_n x49 -> x0, other arithmetic: 15.6 us -> none  [the longest x32 14.5 us: leaf_step(): blocks = jnp.take(leaf_blocks, slots, axis=0)]
    and x22 -> x0, other arithmetic: 11.3 us -> none  [the longest x16 11.3 us: leaf_step(): blocks = jnp.take(leaf_blocks, slots, axis=0)]
    convert_element_type x16 -> x0, other arithmetic: 11 us -> none  [leaf_step(): live.astype(beside_all.dtype)[:, None, None]]
  transfers between devices with their start and end apart: 8 -> 13, of which waited for: 1 -> 8; matrix products, arithmetic and copies ran while one was open for 14% -> 0% of each run, Pallas kernels for 0% -> 32%
where the time goes in v1:
time: 131 us; the launch traced here: 129 us
  Pallas kernels  62.8 us (48%)
  starting transfers between devices  36.5 us (28%)
  local copies, waits for them, and re-layouts  14.9 us (11%)
  waiting for transfers between devices  14.5 us (11%)
    pallas_call x4, Pallas kernels, pairs(): pl.pallas_call(functools.partial(pair_kernel, seg, len(nodes), bool(box),...  51.6 us
    ppermute x9, starting transfers between devices, three_partners(): nodes.append(lax.ppermute(node, 'box', pairs))  24.9 us
    unnamed x46, local copies, waits for them, and re-layouts  14.9 us
    ppermute x9, waiting for transfers between devices, three_partners(): nodes.append(lax.ppermute(node, 'box', pairs))  14.5 us
    pallas_call x1, Pallas kernels, skeleton(): pl.pallas_call(functools.partial(skeleton_kernel, chunk, far_blocks), gri...  8.34 us
    ppermute x2, starting transfers between devices, local(): before = [lax.ppermute(a, 'box', up) for a in (points, weights)]  7.74 us
    ppermute x2, starting transfers between devices, local(): after = [lax.ppermute(a, 'box', down) for a in (points, weights)]  3.85 us
    pallas_call x3, Pallas kernels, climb(): pl.pallas_call(functools.partial(climb_kernel, dim, level, last), out_sha...  2.94 us
  transfers between devices with their start and end apart: 13, of which 8 were waited for; matrix products, arithmetic and copies ran while one was open for 0% of the time, Pallas kernels for 32%

profile of v1, /device:TPU:49, one launch (start us, length us, event | category | flops | bytes accessed | tf_op | source)
XLA Modules:
  0.0 128.9 jit_solution(4692597602375135956)
XLA Ops:
  0.0 4.1 %collective-permute-start.11 = (bf16[64,8192]{1,0:T(8,128)(2,1)}, bf16[64,8192]{1,0:T(8,128)(2,1)}, u32[]{:S(2)}, u32[]{:S(2)}) collective-permute-start(bf16[64,8192]{1,0:T(8,128)(2,1)} %bitcast.6), channel_id=1, source_target_pairs={{0,4},{4,8},{8,12},{12,16},{16,20},{20,24},{24,28},{28,32},{32,36}... | collective-permute-start | bytes 3145736 | tf_op jit(solution)/shard_map/ppermute | solution.py:289
  4.1 1.9 %collective-permute-start.9 = (bf16[64,8192]{1,0:T(8,128)(2,1)}, bf16[64,8192]{1,0:T(8,128)(2,1)}, u32[]{:S(2)}, u32[]{:S(2)}) collective-permute-start(bf16[64,8192]{1,0:T(8,128)(2,1)} %bitcast.7), channel_id=1, source_target_pairs={{4,0},{8,4},{12,8},{16,12},{20,16},{24,20},{28,24},{32,28},{36,32}... | collective-permute-start | bytes 3145736 | tf_op jit(solution)/shard_map/ppermute | solution.py:290
  6.0 3.6 %collective-permute-start.12 = (bf16[32,8192]{1,0:T(8,128)(2,1)}, bf16[32,8192]{1,0:T(8,128)(2,1)}, u32[]{:S(2)}, u32[]{:S(2)}) collective-permute-start(bf16[32,8192]{1,0:T(8,128)(2,1)} %bitcast.14), channel_id=1, source_target_pairs={{0,4},{4,8},{8,12},{12,16},{16,20},{20,24},{24,28},{28,32},{32,36}... | collective-permute-start | bytes 1572872 | tf_op jit(solution)/shard_map/ppermute | solution.py:289
  9.7 1.9 %collective-permute-start.10 = (bf16[32,8192]{1,0:T(8,128)(2,1)}, bf16[32,8192]{1,0:T(8,128)(2,1)}, u32[]{:S(2)}, u32[]{:S(2)}) collective-permute-start(bf16[32,8192]{1,0:T(8,128)(2,1)} %bitcast.15), channel_id=1, source_target_pairs={{4,0},{8,4},{12,8},{16,12},{20,16},{24,20},{28,24},{32,28},{36,32}... | collective-permute-start | bytes 1572872 | tf_op jit(solution)/shard_map/ppermute | solution.py:290
  11.6 1.2 copy-done
  12.8 2.2 %copy-done.3 = bf16[1,256,8192]{2,1,0:T(8,128)(2,1)S(1)} copy-done((bf16[1,256,8192]{2,1,0:T(8,128)(2,1)S(1)}, bf16[1,256,8192]{2,1,0:T(8,128)(2,1)}, u32[]{:S(2)}) %copy-start.3) | copy-done | bytes 4194328
  15.0 1.0 copy-done.4
  18.1 8.3 %skeleton.1 = (bf16[96,256]{1,0:T(8,128)(2,1)S(1)}, s32[3,512]{1,0:T(4,128)S(1)}, s32[3]{0:T(128)S(1)}) custom-call(s32[16,12]{1,0:T(8,128)S(1)} %copy-done.17, s32[16]{0:T(128)S(1)} %copy-done.22, s32[1,256]{1,0:T(1,128)S(1)} %copy-done.21, bf16[64,8192]{1,0:T(8,128)(2,1)S(1)} %bitcast.8, bf16[32,8192]{1,0:T(8,128)(2,1)S(1)} %bitcast.16, ...), custom_call_target="tpu_custom_call" | custom-call | tf_op jit(solution)/shard_map/skeleton/pallas_call | solution.py:95
  27.1 1.2 collective-permute-done.one.refs_5_
  28.3 2.9 %collective-permute-done.1.two = bf16[96,256]{1,0:T(8,128)(2,1)S(1)} collective-permute-done((bf16[96,256]{1,0:T(8,128)(2,1)S(1)}, bf16[96,256]{1,0:T(8,128)(2,1)S(1)}, u32[]{:S(2)}, u32[]{:S(2)}) %collective-permute-start.1) | collective-permute-done | bytes 49184 | tf_op jit(solution)/shard_map/ppermute | solution.py:164
  31.2 1.1 collective-permute-start.2
  32.3 2.4 %collective-permute-done.2.three = bf16[96,256]{1,0:T(8,128)(2,1)S(1)} collective-permute-done((bf16[96,256]{1,0:T(8,128)(2,1)S(1)}, bf16[96,256]{1,0:T(8,128)(2,1)S(1)}, u32[]{:S(2)}, u32[]{:S(2)}) %collective-permute-start.2) | collective-permute-done | bytes 49184 | tf_op jit(solution)/shard_map/ppermute | solution.py:164
  36.0 3.6 %collective-permute-start.3 = (bf16[96,256]{1,0:T(8,128)(2,1)S(1)}, bf16[96,256]{1,0:T(8,128)(2,1)S(1)}, u32[]{:S(2)}, u32[]{:S(2)}) collective-permute-start(bf16[96,256]{1,0:T(8,128)(2,1)S(1)} %get-tuple-element.15.own), channel_id=1, source_target_pairs={{0,16},{4,20},{8,24},{12,28},{16,0},{20,4},{24,8},{28,12},{32,48},... | collective-permute-start | bytes 147464 | tf_op jit(solution)/shard_map/ppermute | solution.py:164
  39.5 1.6 %collective-permute-done.3.one.refs_5_ = bf16[96,256]{1,0:T(8,128)(2,1)S(1)} collective-permute-done((bf16[96,256]{1,0:T(8,128)(2,1)S(1)}, bf16[96,256]{1,0:T(8,128)(2,1)S(1)}, u32[]{:S(2)}, u32[]{:S(2)}) %collective-permute-start.3) | collective-permute-done | bytes 49184 | tf_op jit(solution)/shard_map/ppermute | solution.py:164
  41.1 6.1 %collective-permute-start.4 = (bf16[96,256]{1,0:T(8,128)(2,1)S(1)}, bf16[96,256]{1,0:T(8,128)(2,1)S(1)}, u32[]{:S(2)}, u32[]{:S(2)}) collective-permute-start(bf16[96,256]{1,0:T(8,128)(2,1)S(1)} %get-tuple-element.15.own), channel_id=1, source_target_pairs={{0,32},{4,36},{8,40},{12,44},{16,48},{20,52},{24,56},{28,60},{32,0... | collective-permute-start | bytes 147464 | tf_op jit(solution)/shard_map/ppermute | solution.py:164
  47.2 1.5 %collective-permute-done.4.two = bf16[96,256]{1,0:T(8,128)(2,1)S(1)} collective-permute-done((bf16[96,256]{1,0:T(8,128)(2,1)S(1)}, bf16[96,256]{1,0:T(8,128)(2,1)S(1)}, u32[]{:S(2)}, u32[]{:S(2)}) %collective-permute-start.4) | collective-permute-done | bytes 49184 | tf_op jit(solution)/shard_map/ppermute | solution.py:164
  48.7 4.0 %collective-permute-start.5 = (bf16[96,256]{1,0:T(8,128)(2,1)S(1)}, bf16[96,256]{1,0:T(8,128)(2,1)S(1)}, u32[]{:S(2)}, u32[]{:S(2)}) collective-permute-start(bf16[96,256]{1,0:T(8,128)(2,1)S(1)} %get-tuple-element.15.own), channel_id=1, source_target_pairs={{0,48},{4,52},{8,56},{12,60},{16,32},{20,36},{24,40},{28,44},{32,1... | collective-permute-start | bytes 147464 | tf_op jit(solution)/shard_map/ppermute | solution.py:164
  52.7 1.5 %collective-permute-done.5.three = bf16[96,256]{1,0:T(8,128)(2,1)S(1)} collective-permute-done((bf16[96,256]{1,0:T(8,128)(2,1)S(1)}, bf16[96,256]{1,0:T(8,128)(2,1)S(1)}, u32[]{:S(2)}, u32[]{:S(2)}) %collective-permute-start.5) | collective-permute-done | bytes 49184 | tf_op jit(solution)/shard_map/ppermute | solution.py:164
  54.1 1.2 climb.4
  56.0 2.1 %collective-permute-start.6 = (bf16[96,256]{1,0:T(8,128)(2,1)}, bf16[96,256]{1,0:T(8,128)(2,1)S(1)}, u32[]{:S(2)}, u32[]{:S(2)}) collective-permute-start(bf16[96,256]{1,0:T(8,128)(2,1)} %get-tuple-element.16.own), channel_id=1, source_target_pairs={{0,64},{4,68},{8,72},{12,76},{16,80},{20,84},{24,88},{28,92},{32,9... | collective-permute-start | bytes 147464 | tf_op jit(solution)/shard_map/ppermute | solution.py:164
  58.1 1.7 %collective-permute-done.6.one.refs_3_ = bf16[96,256]{1,0:T(8,128)(2,1)S(1)} collective-permute-done((bf16[96,256]{1,0:T(8,128)(2,1)}, bf16[96,256]{1,0:T(8,128)(2,1)S(1)}, u32[]{:S(2)}, u32[]{:S(2)}) %collective-permute-start.6) | collective-permute-done | bytes 49184 | tf_op jit(solution)/shard_map/ppermute | solution.py:164
  59.8 4.9 %collective-permute-start.7 = (bf16[96,256]{1,0:T(8,128)(2,1)}, bf16[96,256]{1,0:T(8,128)(2,1)S(1)}, u32[]{:S(2)}, u32[]{:S(2)}) collective-permute-start(bf16[96,256]{1,0:T(8,128)(2,1)} %get-tuple-element.16.own), channel_id=1, source_target_pairs={{0,128},{4,132},{8,136},{12,140},{16,144},{20,148},{24,152},{28,15... | collective-permute-start | bytes 147464 | tf_op jit(solution)/shard_map/ppermute | solution.py:164
  64.7 1.7 %collective-permute-done.7.two = bf16[96,256]{1,0:T(8,128)(2,1)S(1)} collective-permute-done((bf16[96,256]{1,0:T(8,128)(2,1)}, bf16[96,256]{1,0:T(8,128)(2,1)S(1)}, u32[]{:S(2)}, u32[]{:S(2)}) %collective-permute-start.7) | collective-permute-done | bytes 49184 | tf_op jit(solution)/shard_map/ppermute | solution.py:164
  67.0 3.2 %collective-permute-start.8 = (bf16[96,256]{1,0:T(8,128)(2,1)}, bf16[96,256]{1,0:T(8,128)(2,1)}, u32[]{:S(2)}, u32[]{:S(2)}) collective-permute-start(bf16[96,256]{1,0:T(8,128)(2,1)} %get-tuple-element.16.own), channel_id=1, source_target_pairs={{0,192},{4,196},{8,200},{12,204},{16,208},{20,212},{24,216},{28,22... | collective-permute-start | bytes 147464 | tf_op jit(solution)/shard_map/ppermute | solution.py:164
  70.2 1.0 copy-done.5
  72.5 14.6 %pairs.4.refs_7_ = f32[32,8192]{1,0:T(8,128)S(1)} custom-call(s32[3,512]{1,0:T(4,128)S(1)} %copy-done.7, s32[3]{0:T(128)S(1)} %copy-done.19, bf16[64,8192]{1,0:T(8,128)(2,1)S(1)} %bitcast.9, bf16[64,8192]{1,0:T(8,128)(2,1)S(1)} %bitcast.10, bf16[32,8192]{1,0:T(8,128)(2,1)S(1)} %bitcast.17), custom_call_target="tpu_custom_call" | custom-call | tf_op jit(solution)/shard_map/pairs/pallas_call | solution.py:266
  87.9 0.8 copy-done.16
  88.7 1.1 climb.5.refs_4_
  90.5 0.8 copy-done.12
  91.9 15.5 %pairs.5.refs_7_ = f32[32,8192]{1,0:T(8,128)S(1)} custom-call(s32[3,512]{1,0:T(4,128)S(1)} %copy-done.8, s32[3]{0:T(128)S(1)} %copy-done.20, bf16[64,8192]{1,0:T(8,128)(2,1)S(1)} %bitcast.11, bf16[64,8192]{1,0:T(8,128)(2,1)} %collective-permute-done.11.refs_3_, bf16[32,8192]{1,0:T(8,128)(2,1)} %collective-permute-done.12.refs_4_, ...), custom_call_target="tpu_custom_call" | custom-call | tf_op jit(solution)/shard_map/pairs/pallas_call | solution.py:266
  107.5 15.5 %pairs.6.refs_5_ = f32[32,8192]{1,0:T(8,128)S(1)} custom-call(s32[3,512]{1,0:T(4,128)S(1)} %copy-done.8, s32[3]{0:T(128)S(1)} %copy-done.20, bf16[64,8192]{1,0:T(8,128)(2,1)S(1)} %bitcast.12, bf16[64,8192]{1,0:T(8,128)(2,1)} %collective-permute-done.9.refs_3_, bf16[32,8192]{1,0:T(8,128)(2,1)} %collective-permute-done.10.refs_4_, ...), custom_call_target="tpu_custom_call" | custom-call | tf_op jit(solution)/shard_map/pairs/pallas_call | solution.py:266
  123.0 5.9 %pairs.7 = bf16[32,8192]{1,0:T(8,128)(2,1)} custom-call(s32[3,512]{1,0:T(4,128)S(1)} %copy-done.8, s32[3]{0:T(128)S(1)} %copy-done.20, bf16[64,8192]{1,0:T(8,128)(2,1)S(1)} %bitcast.13, bf16[96,256]{1,0:T(8,128)(2,1)S(1)} %collective-permute-done.6.one.refs_3_, bf16[96,256]{1,0:T(8,128)(2,1)S(1)} %climb.5.refs_4_, f32[32,8192]{1,0:T(8,128)S(1)} %pairs.6.refs_5_), custom_call_target="tpu_custom_call" | custom-call | tf_op jit(solution)/shard_map/pairs/pallas_call | solution.py:266
  (48 shorter events, 8.4 us)
Async XLA Ops:
  0.0 89.8 %collective-permute-start.11 = (bf16[64,8192]{1,0:T(8,128)(2,1)}, bf16[64,8192]{1,0:T(8,128)(2,1)}, u32[]{:S(2)}, u32[]{:S(2)}) collective-permute-start(bf16[64,8192]{1,0:T(8,128)(2,1)} %bitcast.6), channel_id=1, source_target_pairs={{0,4},{4,8},{8,12},{12,16},{16,20},{20,24},{24,28},{28,32},{32,36}... | collective-permute-start | bytes 3145736 | tf_op jit(solution)/shard_map/ppermute | solution.py:289
  4.1 103.3 %collective-permute-start.9 = (bf16[64,8192]{1,0:T(8,128)(2,1)}, bf16[64,8192]{1,0:T(8,128)(2,1)}, u32[]{:S(2)}, u32[]{:S(2)}) collective-permute-start(bf16[64,8192]{1,0:T(8,128)(2,1)} %bitcast.7), channel_id=1, source_target_pairs={{4,0},{8,4},{12,8},{16,12},{20,16},{24,20},{28,24},{32,28},{36,32}... | collective-permute-start | bytes 3145736 | tf_op jit(solution)/shard_map/ppermute | solution.py:290
  6.0 83.7 %collective-permute-start.12 = (bf16[32,8192]{1,0:T(8,128)(2,1)}, bf16[32,8192]{1,0:T(8,128)(2,1)}, u32[]{:S(2)}, u32[]{:S(2)}) collective-permute-start(bf16[32,8192]{1,0:T(8,128)(2,1)} %bitcast.14), channel_id=1, source_target_pairs={{0,4},{4,8},{8,12},{12,16},{16,20},{20,24},{24,28},{28,32},{32,36}... | collective-permute-start | bytes 1572872 | tf_op jit(solution)/shard_map/ppermute | solution.py:289
  9.7 97.8 %collective-permute-start.10 = (bf16[32,8192]{1,0:T(8,128)(2,1)}, bf16[32,8192]{1,0:T(8,128)(2,1)}, u32[]{:S(2)}, u32[]{:S(2)}) collective-permute-start(bf16[32,8192]{1,0:T(8,128)(2,1)} %bitcast.15), channel_id=1, source_target_pairs={{4,0},{8,4},{12,8},{16,12},{20,16},{24,20},{28,24},{32,28},{36,32}... | collective-permute-start | bytes 1572872 | tf_op jit(solution)/shard_map/ppermute | solution.py:290
  11.6 1.2 copy-start
  12.8 2.2 %copy-start.3 = (bf16[1,256,8192]{2,1,0:T(8,128)(2,1)S(1)}, bf16[1,256,8192]{2,1,0:T(8,128)(2,1)}, u32[]{:S(2)}) copy-start(bf16[1,256,8192]{2,1,0:T(8,128)(2,1)} %maps.4) | copy-start | bytes 12582916
  15.0 1.0 copy-start.4
  16.1 0.7 copy-start.17
  16.8 0.7 copy-start.21
  17.5 0.7 copy-start.22
  18.1 16.6 %copy-start.2 = (bf16[5,256,512]{2,1,0:T(8,128)(2,1)S(1)}, bf16[5,256,512]{2,1,0:T(8,128)(2,1)}, u32[]{:S(2)}) copy-start(bf16[5,256,512]{2,1,0:T(8,128)(2,1)} %maps.7) | copy-start | bytes 3932164
  18.1 16.6 %copy-start.9 = (s32[5,256]{1,0:T(8,128)S(1)}, s32[5,256]{1,0:T(8,128)}, u32[]{:S(2)}) copy-start(s32[5,256]{1,0:T(8,128)} %index.7) | copy-start | bytes 15364
  18.1 52.1 %copy-start.1 = (bf16[8192,64]{0,1:T(8,128)(2,1)S(1)}, bf16[8192,64]{0,1:T(8,128)(2,1)}, u32[]{:S(2)}) copy-start(bf16[8192,64]{0,1:T(8,128)(2,1)} %param.8) | copy-start | bytes 3145732
  27.1 4.2 %copy-start.18 = (s32[3]{0:T(128)}, s32[3]{0:T(128)S(1)}, u32[]{:S(2)}) copy-start(s32[3]{0:T(128)S(1)} %get-tuple-element.13.refs_1_) | copy-start | bytes 40
  27.1 1.2 collective-permute-start
  28.3 2.9 %collective-permute-start.1 = (bf16[96,256]{1,0:T(8,128)(2,1)S(1)}, bf16[96,256]{1,0:T(8,128)(2,1)S(1)}, u32[]{:S(2)}, u32[]{:S(2)}) collective-permute-start(bf16[96,256]{1,0:T(8,128)(2,1)S(1)} %get-tuple-element.14.own), channel_id=1, source_target_pairs={{0,8},{4,12},{8,0},{12,4},{16,24},{20,28},{24,16},{28,20},{32,40},... | collective-permute-start | bytes 147464 | tf_op jit(solution)/shard_map/ppermute | solution.py:164
  31.2 3.5 %collective-permute-start.2 = (bf16[96,256]{1,0:T(8,128)(2,1)S(1)}, bf16[96,256]{1,0:T(8,128)(2,1)S(1)}, u32[]{:S(2)}, u32[]{:S(2)}) collective-permute-start(bf16[96,256]{1,0:T(8,128)(2,1)S(1)} %get-tuple-element.14.own), channel_id=1, source_target_pairs={{0,12},{4,8},{8,4},{12,0},{16,28},{20,24},{24,20},{28,16},{32,44},... | collective-permute-start | bytes 147464 | tf_op jit(solution)/shard_map/ppermute | solution.py:164
  35.3 0.6 copy-start.11
  36.0 5.1 %collective-permute-start.3 = (bf16[96,256]{1,0:T(8,128)(2,1)S(1)}, bf16[96,256]{1,0:T(8,128)(2,1)S(1)}, u32[]{:S(2)}, u32[]{:S(2)}) collective-permute-start(bf16[96,256]{1,0:T(8,128)(2,1)S(1)} %get-tuple-element.15.own), channel_id=1, source_target_pairs={{0,16},{4,20},{8,24},{12,28},{16,0},{20,4},{24,8},{28,12},{32,48},... | collective-permute-start | bytes 147464 | tf_op jit(solution)/shard_map/ppermute | solution.py:164
  41.1 7.6 %collective-permute-start.4 = (bf16[96,256]{1,0:T(8,128)(2,1)S(1)}, bf16[96,256]{1,0:T(8,128)(2,1)S(1)}, u32[]{:S(2)}, u32[]{:S(2)}) collective-permute-start(bf16[96,256]{1,0:T(8,128)(2,1)S(1)} %get-tuple-element.15.own), channel_id=1, source_target_pairs={{0,32},{4,36},{8,40},{12,44},{16,48},{20,52},{24,56},{28,60},{32,0... | collective-permute-start | bytes 147464 | tf_op jit(solution)/shard_map/ppermute | solution.py:164
  48.7 5.4 %collective-permute-start.5 = (bf16[96,256]{1,0:T(8,128)(2,1)S(1)}, bf16[96,256]{1,0:T(8,128)(2,1)S(1)}, u32[]{:S(2)}, u32[]{:S(2)}) collective-permute-start(bf16[96,256]{1,0:T(8,128)(2,1)S(1)} %get-tuple-element.15.own), channel_id=1, source_target_pairs={{0,48},{4,52},{8,56},{12,60},{16,32},{20,36},{24,40},{28,44},{32,1... | collective-permute-start | bytes 147464 | tf_op jit(solution)/shard_map/ppermute | solution.py:164
  56.0 3.8 %collective-permute-start.6 = (bf16[96,256]{1,0:T(8,128)(2,1)}, bf16[96,256]{1,0:T(8,128)(2,1)S(1)}, u32[]{:S(2)}, u32[]{:S(2)}) collective-permute-start(bf16[96,256]{1,0:T(8,128)(2,1)} %get-tuple-element.16.own), channel_id=1, source_target_pairs={{0,64},{4,68},{8,72},{12,76},{16,80},{20,84},{24,88},{28,92},{32,9... | collective-permute-start | bytes 147464 | tf_op jit(solution)/shard_map/ppermute | solution.py:164
  59.8 6.6 %collective-permute-start.7 = (bf16[96,256]{1,0:T(8,128)(2,1)}, bf16[96,256]{1,0:T(8,128)(2,1)S(1)}, u32[]{:S(2)}, u32[]{:S(2)}) collective-permute-start(bf16[96,256]{1,0:T(8,128)(2,1)} %get-tuple-element.16.own), channel_id=1, source_target_pairs={{0,128},{4,132},{8,136},{12,140},{16,144},{20,148},{24,152},{28,15... | collective-permute-start | bytes 147464 | tf_op jit(solution)/shard_map/ppermute | solution.py:164
  66.4 0.6 copy-start.15
  67.0 20.2 %collective-permute-start.8 = (bf16[96,256]{1,0:T(8,128)(2,1)}, bf16[96,256]{1,0:T(8,128)(2,1)}, u32[]{:S(2)}, u32[]{:S(2)}) collective-permute-start(bf16[96,256]{1,0:T(8,128)(2,1)} %get-tuple-element.16.own), channel_id=1, source_target_pairs={{0,192},{4,196},{8,200},{12,204},{16,208},{20,212},{24,216},{28,22... | collective-permute-start | bytes 147464 | tf_op jit(solution)/shard_map/ppermute | solution.py:164
  70.2 1.0 copy-start.5
  71.2 0.7 copy-start.7
  87.1 0.7 copy-start.10
  87.8 0.8 copy-start.16
  88.6 18.8 %copy-start.14 = (bf16[96,256]{1,0:T(8,128)(2,1)S(1)}, bf16[96,256]{1,0:T(8,128)(2,1)}, u32[]{:S(2)}) copy-start(bf16[96,256]{1,0:T(8,128)(2,1)} %copy-done.13) | copy-start | bytes 147460
  89.8 0.7 copy-start.8
  90.5 0.8 copy-start.12
  (4 other events, 2.4 us)

commit v2 on v0

v2 whole, which is shorter than its diff:
```python
import functools

import jax
import jax.numpy as jnp
from jax import lax
from jax.experimental import pallas as pl
from jax.experimental.pallas import tpu as pltpu
from jax.sharding import PartitionSpec as P

LEAF = 512
HALF = 256
UNROLL = 16
AHEAD = 2
LIST = 256
DEPTH = 80
ROW_BITS = 5
CHUNKS = 8
VMEM = 14 * 2**20
F32 = jnp.float32
BF16 = jnp.bfloat16
NT = (((1,), (1,)), ((), ()))
TN = (((0,), (0,)), ((), ()))


def in_vmem():
    return pl.BlockSpec(memory_space=pltpu.VMEM)


def in_smem():
    return pl.BlockSpec(memory_space=pltpu.SMEM)


def params():
    return pltpu.CompilerParams(vmem_limit_bytes=VMEM)


def cost(microseconds):
    return pl.CostEstimate(
        flops=int(microseconds * 10**9), bytes_accessed=int(microseconds * 10**6), transcendentals=0
    )


def pieces(points):
    wide = points.astype(F32)
    norm = jnp.sum(wide * wide, axis=0, keepdims=True) * (2.0 / points.shape[0])
    high = norm.astype(BF16).astype(F32)
    middle = (norm - high).astype(BF16).astype(F32)
    low = norm - high - middle
    scaled = (wide * (4.0 / points.shape[0]) ** 0.5).astype(BF16)
    return scaled, high, middle, low


def extended(points, of_rows):
    scaled, high, middle, low = pieces(points)
    first = 0 if of_rows else 3
    row = lax.broadcasted_iota(jnp.int32, (16, points.shape[1]), 0)
    norm = jnp.where(row == first, -high, jnp.where(row == first + 1, -middle, -low))
    is_norm = (row >= first) & (row < first + 3)
    return scaled, jnp.where(is_norm, norm, jnp.where(row < 6, 1.0, 0.0)).astype(BF16)


def put(target, at, points, of_rows):
    scaled, norm = extended(points, of_rows)
    dim = points.shape[0]
    target[:dim, at] = scaled
    target[dim:, at] = norm


def level_0_kernel(dim, near_list, near_count, index, both, maps, node, lists, counts, rows, centers):
    columns, width = both.shape[0] - dim, both.shape[1]
    leaves, slots = near_list.shape
    size = index.shape[1]
    rows[:, width:] = jnp.zeros((DEPTH, LEAF), BF16)
    coords = jnp.zeros((dim, size), F32)
    values = jnp.zeros((size, columns), F32)
    ends = [jnp.int32(s * LIST) for s in range(3)]
    chunk = width // CHUNKS
    for start in range(0, width, chunk):
        at = pl.ds(start, chunk)
        points = both[:dim, at]
        place = lax.broadcasted_iota(jnp.int32, (chunk, size), 0) + start
        pick = jnp.where(place == index[...], 1.0, 0.0).astype(BF16)
        coords += jnp.dot(points, pick, preferred_element_type=F32)
        values += lax.dot_general(maps[0, :, at], both[dim:, at], NT, preferred_element_type=F32)
        put(rows, at, points, True)
        put(centers, at, points, False)
        for leaf in range(start // LEAF, (start + chunk) // LEAF):
            live = near_count[leaf]
            for k in range(slots):
                slot = near_list[leaf, k]
                used = k < live
                low, mid = slot < leaves, slot < 2 * leaves
                to = jnp.where(low, ends[0], jnp.where(mid, ends[1], ends[2]))
                to = jnp.where(used, to, 3 * LIST)
                lists[to] = jnp.bitwise_and(slot, leaves - 1) * 2**ROW_BITS + leaf
                used = used.astype(jnp.int32)
                is_low, is_mid = low.astype(jnp.int32), mid.astype(jnp.int32)
                ends[0] += is_low * used
                ends[1] += (is_mid - is_low) * used
                ends[2] += (1 - is_mid) * used
    for s in range(3):
        counts[s] = ends[s] - s * LIST
        for pad in range(UNROLL // 2):
            lists[ends[s] + pad] = leaves
    node[:dim, :] = coords.astype(BF16)
    node[dim:, :] = values.T.astype(BF16)


def level_0(both, near_list, near_count, index, maps, dim):
    total, width = both.shape
    columns = total - dim
    size = index.shape[1]
    return pl.pallas_call(
        functools.partial(level_0_kernel, dim),
        out_shape=(
            jax.ShapeDtypeStruct((total, size), BF16),
            jax.ShapeDtypeStruct((3 * LIST + 8,), jnp.int32),
            jax.ShapeDtypeStruct((3,), jnp.int32),
            jax.ShapeDtypeStruct((DEPTH, width + LEAF), BF16),
            jax.ShapeDtypeStruct((DEPTH, width), BF16),
        ),
        in_specs=[in_smem(), in_smem(), in_vmem(), in_vmem(), in_vmem()],
        out_specs=(in_vmem(), in_smem(), in_smem(), in_vmem(), in_vmem()),
        compiler_params=params(),
        cost_estimate=cost(1),
        name="level_0",
    )(near_list, near_count, index, both, maps)


def climb_kernel(dim, level, position, index, maps, own, other, *refs):
    parent = refs[-1]
    is_upper = jnp.bitwise_and(jnp.right_shift(position[0], level), 1) == 1
    mine, theirs = own[...].astype(F32), other[...].astype(F32)
    lower = jnp.where(is_upper, theirs, mine).astype(BF16)
    upper = jnp.where(is_upper, mine, theirs).astype(BF16)
    union = jnp.concatenate([lower, upper], axis=1)
    here = index[level : level + 1, :]
    place = lax.broadcasted_iota(jnp.int32, (union.shape[1], here.shape[1]), 0)
    pick = jnp.where(place == here, 1.0, 0.0).astype(BF16)
    parent[:dim, :] = jnp.dot(union[:dim], pick, preferred_element_type=F32).astype(BF16)
    merged = lax.dot_general(union[dim:], maps[level], NT, preferred_element_type=F32)
    parent[dim:, :] = merged.astype(BF16)


def climb(dim, level, position, index, maps, own, other, after):
    order = [] if after is None else [after]
    return pl.pallas_call(
        functools.partial(climb_kernel, dim, level),
        out_shape=jax.ShapeDtypeStruct(own.shape, BF16),
        in_specs=[in_smem()] + [in_vmem()] * (4 + len(order)),
        out_specs=in_vmem(),
        compiler_params=params(),
        cost_estimate=cost(0.6),
        name="climb",
    )(jnp.reshape(position, (1,)).astype(jnp.int32), index, maps, own, other, *order)


def run(items):
    def exponents(item):
        (centers, at), _, (rows, to), _ = item
        return lax.dot_general(centers[:, at], rows[:, to], TN, preferred_element_type=F32)

    ahead = [exponents(item) for item in items[:AHEAD]]
    for n, (_, (values, at, first), _, (total, to)) in enumerate(items):
        kern = jnp.exp(ahead[n]).astype(BF16)
        if n + AHEAD < len(items):
            ahead.append(exponents(items[n + AHEAD]))
        total[:, to] += jnp.dot(values[first:, at], kern, preferred_element_type=F32)


def pair_kernel(dim, seg, piece, of, ready, has_start, *refs):
    refs = list(refs)
    lists, counts, rows, box = refs[:4]
    del refs[:4]
    centers = refs.pop(0) if ready else None
    node = refs.pop(0)
    start = refs.pop(0) if has_start else None
    total = refs.pop(0)
    far = refs.pop(0)
    if not ready:
        centers = refs.pop(0)

        def fill(i, _):
            at = pl.ds(pl.multiple_of(i * LEAF, LEAF), LEAF)
            put(centers, at, box[:dim, at], False)
            return 0

        lax.fori_loop(0, box.shape[1] // LEAF, fill, 0)
    leaves = box.shape[1] // LEAF
    put(far, pl.ds(0, HALF), node[:dim, :], False)
    total[...] = start[...] if has_start else jnp.zeros_like(total)
    everything = pl.ds(0, HALF)
    run([
        ((far, everything), (node, everything, dim), (rows, pl.ds(leaf * LEAF, LEAF)), (total, pl.ds(leaf * LEAF, LEAF)))
        for leaf in range(leaves)
    ])

    def body(i, _):
        items = []
        for n in range(UNROLL // 2):
            item = lists[seg * LIST + i * (UNROLL // 2) + n]
            source, leaf = jnp.right_shift(item, ROW_BITS), jnp.bitwise_and(item, 2**ROW_BITS - 1)
            to = pl.ds(pl.multiple_of(leaf * LEAF, LEAF), LEAF)
            for half in range(0, LEAF, HALF):
                at = pl.ds(pl.multiple_of(source * LEAF + half, HALF), HALF)
                items.append(((centers, at), (box, at, dim), (rows, to), (total, to)))
        run(items)
        return 0

    rounds = (counts[seg] + UNROLL // 2 - 1) // (UNROLL // 2)
    lax.fori_loop(rounds * piece // of, rounds * (piece + 1) // of, body, 0)


def pairs(dim, seg, piece, of, lists, counts, rows, box, centers, node, start):
    width = box.shape[1]
    columns = box.shape[0] - dim
    ready = centers is not None
    args = [lists, counts, rows, box] + ([centers] if ready else []) + [node]
    args += [] if start is None else [start]
    return pl.pallas_call(
        functools.partial(pair_kernel, dim, seg, piece, of, ready, start is not None),
        out_shape=jax.ShapeDtypeStruct((columns, width + LEAF), F32),
        in_specs=[in_smem(), in_smem()] + [in_vmem()] * (len(args) - 2),
        out_specs=in_vmem(),
        scratch_shapes=[pltpu.VMEM((DEPTH, HALF), BF16)]
        + ([] if ready else [pltpu.VMEM((DEPTH, width), BF16)]),
        compiler_params=params(),
        cost_estimate=cost(4),
        name="pairs",
    )(*args)


def last_kernel(dim, rows, node, start, out, far, total):
    width = out.shape[1]
    put(far, pl.ds(0, HALF), node[:dim, :], False)
    total[...] = start[:, :width]
    everything = pl.ds(0, HALF)
    run([
        ((far, everything), (node, everything, dim), (rows, pl.ds(at, LEAF)), (total, pl.ds(at, LEAF)))
        for at in range(0, width, LEAF)
    ])
    out[...] = total[...].astype(BF16)


def last(dim, rows, node, start):
    columns, width = start.shape[0], start.shape[1] - LEAF
    return pl.pallas_call(
        functools.partial(last_kernel, dim),
        out_shape=jax.ShapeDtypeStruct((columns, width), BF16),
        in_specs=[in_vmem()] * 3,
        out_specs=in_vmem(),
        scratch_shapes=[pltpu.VMEM((DEPTH, HALF), BF16), pltpu.VMEM((columns, width), F32)],
        compiler_params=params(),
        cost_estimate=cost(3),
        name="last",
    )(rows, node, start)


def local(points, weights, near_list, near_count, skeleton_index, skeleton_maps, level_index, level_maps):
    dim = points.shape[1]
    both = jnp.concatenate([points.T, weights.T], axis=0)
    count = lax.axis_size("box")
    position = lax.axis_index("box")
    before = lax.ppermute(both, "box", [(i, i + 1) for i in range(count - 1)])
    after = lax.ppermute(both, "box", [(i + 1, i) for i in range(count - 1)])
    node, lists, counts, rows, centers = level_0(
        both, near_list, near_count, skeleton_index, skeleton_maps, dim
    )

    def sibling(node, level):
        return lax.ppermute(node, "box", [(i, i ^ (1 << level)) for i in range(count)])

    plan = [
        (1, 0, 3, both, centers),
        (1, 1, 3, both, centers),
        (0, 0, 1, before, None),
        (2, 0, 1, after, None),
        (1, 2, 3, both, centers),
    ]
    total = None
    other = sibling(node, 0)
    for level, (seg, piece, of, box, ready) in enumerate(plan):
        node = climb(dim, level, position, level_index, level_maps, node, other, total)
        far = other
        other = sibling(node, level + 1)
        total = pairs(dim, seg, piece, of, lists, counts, rows, box, ready, far, total)
    return last(dim, rows, other, total).T


def solution(mesh):
    return jax.shard_map(
        local,
        mesh=mesh,
        in_specs=(
            P("box", None),
            P("box", "rhs"),
            P("box", None),
            P("box"),
            P("box", None),
            P("box", None, None),
            P(),
            P(),
        ),
        out_specs=P("box", "rhs"),
        check_vma=False,
    )
```

time: 339 us -> 72.6 us (0.21)
  the two profiles are of different devices: /device:TPU:49 before, /device:TPU:35 now
where the time goes in v2:
time: 72.6 us
  Pallas kernels  38.2 us (53%)
  starting transfers between devices  25.9 us (36%)
  local copies, waits for them, and re-layouts  5.73 us (8%)
  other arithmetic  1.53 us (2%)
  waiting for transfers between devices  1.05 us (1%)
    pallas_call x5, Pallas kernels, pairs(): pl.pallas_call(functools.partial(pair_kernel, dim, seg, piece, of, ready,...  29.6 us
    ppermute x6, starting transfers between devices, sibling(): lax.ppermute(node, 'box', [(i, i ^ 1 << level) for i in range(count)])  19.7 us
    unnamed x22, local copies, waits for them, and re-layouts  5.73 us
    pallas_call x1, Pallas kernels, level_0(): pl.pallas_call(functools.partial(level_0_kernel, dim), out_shape=(jax.Sha...  4.84 us
    ppermute x1, starting transfers between devices, local(): before = lax.ppermute(both, 'box', [(i, i + 1) for i in range(count - 1)])  4.24 us
    pallas_call x1, Pallas kernels, last(): pl.pallas_call(functools.partial(last_kernel, dim), out_shape=jax.ShapeDt...  2.39 us
    ppermute x1, starting transfers between devices, local(): after = lax.ppermute(both, 'box', [(i + 1, i) for i in range(count - 1)])  1.92 us
    concatenate x1, other arithmetic, local(): both = jnp.concatenate([points.T, weights.T], axis=0)  1.53 us
  transfers between devices with their start and end apart: 8, of which 1 were waited for; matrix products, arithmetic and copies ran while one was open for 0% of the time, Pallas kernels for 49%

profile of v2, /device:TPU:35, one launch (start us, length us, event | category | flops | bytes accessed | tf_op | source)
XLA Modules:
  0.0 72.6 jit_solution(10051307945584686778)
XLA Ops:
  0.0 1.5 %pad_maximum_fusion.both.refs_3_ = bf16[96,8192]{1,0:T(8,128)(2,1)S(1)} fusion(bf16[32,8192]{1,0:T(8,128)(2,1)} %bitcast.5, bf16[64,8192]{1,0:T(8,128)(2,1)} %bitcast.4), kind=kLoop, calls=%fused_computation | loop fusion | flops 3145728 | bytes 3145728 | tf_op jit(solution)/shard_map/concatenate | solution.py:261
  1.6 0.0 copy-start
  1.6 4.2 %collective-permute-start.4 = (bf16[96,8192]{1,0:T(8,128)(2,1)S(1)}, bf16[96,8192]{1,0:T(8,128)(2,1)}, u32[]{:S(2)}, u32[]{:S(2)}) collective-permute-start(bf16[96,8192]{1,0:T(8,128)(2,1)S(1)} %pad_maximum_fusion.both.refs_3_), channel_id=1, source_target_pairs={{0,4},{4,8},{8,12},{12,16},{16,20},{20,24},{24,28},{28,32},{32,36}... | collective-permute-start | bytes 4718600 | tf_op jit(solution)/shard_map/ppermute | solution.py:264
  5.8 1.9 %collective-permute-start.6 = (bf16[96,8192]{1,0:T(8,128)(2,1)S(1)}, bf16[96,8192]{1,0:T(8,128)(2,1)}, u32[]{:S(2)}, u32[]{:S(2)}) collective-permute-start(bf16[96,8192]{1,0:T(8,128)(2,1)S(1)} %pad_maximum_fusion.both.refs_3_), channel_id=1, source_target_pairs={{4,0},{8,4},{12,8},{16,12},{20,16},{24,20},{28,24},{32,28},{36,32}... | collective-permute-start | bytes 4718600 | tf_op jit(solution)/shard_map/ppermute | solution.py:265
  7.8 0.0 copy-start.1
  7.8 2.2 %copy-done.1 = bf16[1,256,8192]{2,1,0:T(8,128)(2,1)S(1)} copy-done((bf16[1,256,8192]{2,1,0:T(8,128)(2,1)S(1)}, bf16[1,256,8192]{2,1,0:T(8,128)(2,1)}, u32[]{:S(2)}) %copy-start.1) | copy-done | bytes 4194328
  10.0 4.8 %level_0.1 = (bf16[96,256]{1,0:T(8,128)(2,1)S(1)}, s32[776]{0:T(1024)S(1)}, s32[3]{0:T(128)S(1)}, bf16[80,8704]{1,0:T(8,128)(2,1)S(1)}, bf16[80,8192]{1,0:T(8,128)(2,1)S(1)}) custom-call(s32[16,12]{1,0:T(8,128)S(1)} %copy-done.3, s32[16]{0:T(128)S(1)} %copy-done.5, s32[1,256]{1,0:T(1,128)S(1)} %copy-done.4, ...), custom_call_target="tpu_custom_call" | custom-call | flops 1000000000 | bytes 1000000 | tf_op jit(solution)/shard_map/level_0/pallas_call | solution.py:113
  14.8 1.1 %copy-done.6 = bf16[80,8704]{1,0:T(8,128)(2,1)} copy-done((bf16[80,8704]{1,0:T(8,128)(2,1)}, bf16[80,8704]{1,0:T(8,128)(2,1)S(1)}, u32[]{:S(2)}) %copy-start.6) | copy-done | bytes 1392664
  15.9 1.1 %copy-done.8 = bf16[80,8192]{1,0:T(8,128)(2,1)} copy-done((bf16[80,8192]{1,0:T(8,128)(2,1)}, bf16[80,8192]{1,0:T(8,128)(2,1)S(1)}, u32[]{:S(2)}) %copy-start.8) | copy-done | bytes 1310744
  17.0 0.2 collective-permute-start
  17.2 1.0 %collective-permute-done.other.refs_5_ = bf16[96,256]{1,0:T(8,128)(2,1)S(1)} collective-permute-done((bf16[96,256]{1,0:T(8,128)(2,1)S(1)}, bf16[96,256]{1,0:T(8,128)(2,1)S(1)}, u32[]{:S(2)}, u32[]{:S(2)}) %collective-permute-start) | collective-permute-done | bytes 49184 | tf_op jit(solution)/shard_map/ppermute | solution.py:271
  18.3 0.3 climb.5.own
  18.5 3.3 %collective-permute-start.1 = (bf16[96,256]{1,0:T(8,128)(2,1)S(1)}, bf16[96,256]{1,0:T(8,128)(2,1)S(1)}, u32[]{:S(2)}, u32[]{:S(2)}) collective-permute-start(bf16[96,256]{1,0:T(8,128)(2,1)S(1)} %climb.5.own), channel_id=1, source_target_pairs={{0,8},{4,12},{8,0},{12,4},{16,24},{20,28},{24,16},{28,20},{32,40},... | collective-permute-start | bytes 147464 | tf_op jit(solution)/shard_map/ppermute | solution.py:271
  21.8 1.3 %copy-done.9 = bf16[80,8192]{1,0:T(8,128)(2,1)S(1)} copy-done((bf16[80,8192]{1,0:T(8,128)(2,1)S(1)}, bf16[80,8192]{1,0:T(8,128)(2,1)}, u32[]{:S(2)}) %copy-start.9) | copy-done | bytes 1310744
  23.1 3.8 %pairs.5.refs_0_.refs_6_ = f32[32,8704]{1,0:T(8,128)S(1)} custom-call(s32[776]{0:T(1024)S(1)} %get-tuple-element.12.refs_0_, s32[3]{0:T(128)S(1)} %get-tuple-element.13.refs_1_, bf16[80,8704]{1,0:T(8,128)(2,1)S(1)} %copy-done.7, bf16[96,8192]{1,0:T(8,128)(2,1)S(1)} %pad_maximum_fusion.both.refs_3_, bf16[80,8192]{1,0:T(8,128)(2,1)S(1)} %copy-done.9, ...), custom_call_target="tpu_custom_call" | custom-call | flops 4000000000 | bytes 4000000 | tf_op jit(solution)/shard_map/pairs/pallas_call | solution.py:220
  26.9 0.0 collective-permute-done.1.other.refs_5_
  26.9 0.3 climb.6.own
  27.2 1.0 %collective-permute-start.2 = (bf16[96,256]{1,0:T(8,128)(2,1)S(1)}, bf16[96,256]{1,0:T(8,128)(2,1)S(1)}, u32[]{:S(2)}, u32[]{:S(2)}) collective-permute-start(bf16[96,256]{1,0:T(8,128)(2,1)S(1)} %climb.6.own), channel_id=1, source_target_pairs={{0,16},{4,20},{8,24},{12,28},{16,0},{20,4},{24,8},{28,12},{32,48},... | collective-permute-start | bytes 147464 | tf_op jit(solution)/shard_map/ppermute | solution.py:271
  28.2 3.8 %pairs.6.refs_0_.refs_5_ = f32[32,8704]{1,0:T(8,128)S(1)} custom-call(s32[776]{0:T(1024)S(1)} %get-tuple-element.12.refs_0_, s32[3]{0:T(128)S(1)} %get-tuple-element.13.refs_1_, bf16[80,8704]{1,0:T(8,128)(2,1)S(1)} %copy-done.7, bf16[96,8192]{1,0:T(8,128)(2,1)S(1)} %pad_maximum_fusion.both.refs_3_, bf16[80,8192]{1,0:T(8,128)(2,1)S(1)} %copy-done.9, ...), custom_call_target="tpu_custom_call" | custom-call | flops 4000000000 | bytes 4000000 | tf_op jit(solution)/shard_map/pairs/pallas_call | solution.py:220
  32.0 0.0 collective-permute-done.2.other.refs_4_
  32.0 0.3 climb.7.own
  32.3 7.0 %collective-permute-start.3 = (bf16[96,256]{1,0:T(8,128)(2,1)S(1)}, bf16[96,256]{1,0:T(8,128)(2,1)S(1)}, u32[]{:S(2)}, u32[]{:S(2)}) collective-permute-start(bf16[96,256]{1,0:T(8,128)(2,1)S(1)} %climb.7.own), channel_id=1, source_target_pairs={{0,32},{4,36},{8,40},{12,44},{16,48},{20,52},{24,56},{28,60},{32,0... | collective-permute-start | bytes 147464 | tf_op jit(solution)/shard_map/ppermute | solution.py:271
  39.3 0.0 collective-permute-done.4.refs_3_
  39.3 8.4 %pairs.7.refs_0_.refs_5_ = f32[32,8704]{1,0:T(8,128)S(1)} custom-call(s32[776]{0:T(1024)S(1)} %get-tuple-element.12.refs_0_, s32[3]{0:T(128)S(1)} %get-tuple-element.13.refs_1_, bf16[80,8704]{1,0:T(8,128)(2,1)S(1)} %copy-done.7, bf16[96,8192]{1,0:T(8,128)(2,1)} %collective-permute-done.4.refs_3_, bf16[96,256]{1,0:T(8,128)(2,1)S(1)} %collective-permute-done.2.other.refs_4_, ...), custom_call_target="tpu_custom_call" | custom-call | flops 4000000000 | bytes 4000000 | tf_op jit(solution)/shard_map/pairs/pallas_call | solution.py:220
  47.6 0.3 climb.8.own
  47.9 0.1 collective-permute-start.5
  48.0 8.4 %pairs.8.refs_0_.refs_6_ = f32[32,8704]{1,0:T(8,128)S(1)} custom-call(s32[776]{0:T(1024)S(1)} %get-tuple-element.12.refs_0_, s32[3]{0:T(128)S(1)} %get-tuple-element.13.refs_1_, bf16[80,8704]{1,0:T(8,128)(2,1)S(1)} %copy-done.7, bf16[96,8192]{1,0:T(8,128)(2,1)} %collective-permute-done.6.refs_3_, bf16[96,256]{1,0:T(8,128)(2,1)S(1)} %collective-permute-done.3.other.refs_4_, ...), custom_call_target="tpu_custom_call" | custom-call | flops 4000000000 | bytes 4000000 | tf_op jit(solution)/shard_map/pairs/pallas_call | solution.py:220
  56.4 0.3 climb.9
  56.7 8.2 %collective-permute-start.7 = (bf16[96,256]{1,0:T(8,128)(2,1)S(1)}, bf16[96,256]{1,0:T(8,128)(2,1)S(1)}, u32[]{:S(2)}, u32[]{:S(2)}) collective-permute-start(bf16[96,256]{1,0:T(8,128)(2,1)S(1)} %climb.9), channel_id=1, source_target_pairs={{0,128},{4,132},{8,136},{12,140},{16,144},{20,148},{24,152},{28,15... | collective-permute-start | bytes 147464 | tf_op jit(solution)/shard_map/ppermute | solution.py:271
  64.9 5.3 %pairs.9.start = f32[32,8704]{1,0:T(8,128)S(1)} custom-call(s32[776]{0:T(1024)S(1)} %get-tuple-element.12.refs_0_, s32[3]{0:T(128)S(1)} %get-tuple-element.13.refs_1_, bf16[80,8704]{1,0:T(8,128)(2,1)S(1)} %copy-done.7, bf16[96,8192]{1,0:T(8,128)(2,1)S(1)} %pad_maximum_fusion.both.refs_3_, bf16[80,8192]{1,0:T(8,128)(2,1)S(1)} %copy-done.10, ...), custom_call_target="tpu_custom_call" | custom-call | flops 4000000000 | bytes 4000000 | tf_op jit(solution)/shard_map/pairs/pallas_call | solution.py:220
  70.2 0.0 collective-permute-done.7.node
  70.2 2.4 %last.1 = bf16[32,8192]{1,0:T(8,128)(2,1)} custom-call(bf16[80,8704]{1,0:T(8,128)(2,1)S(1)} %copy-done.7, bf16[96,256]{1,0:T(8,128)(2,1)S(1)} %collective-permute-done.7.node, f32[32,8704]{1,0:T(8,128)S(1)} %pairs.9.start), custom_call_target="tpu_custom_call" | custom-call | flops 3000000000 | bytes 3000000 | tf_op jit(solution)/shard_map/last/pallas_call | solution.py:247
  (19 shorter events, 0.0 us)
Async XLA Ops:
  0.0 7.7 %copy-start.3 = (s32[16,12]{1,0:T(8,128)S(1)}, s32[16,12]{1,0:T(8,128)}, u32[]{:S(2)}) copy-start(s32[16,12]{1,0:T(8,128)} %near_list.1) | copy-start | bytes 2308
  0.0 7.7 %copy-start.4 = (s32[1,256]{1,0:T(1,128)S(1)}, s32[1,256]{1,0:T(1,128)}, u32[]{:S(2)}) copy-start(s32[1,256]{1,0:T(1,128)} %index.6) | copy-start | bytes 3076
  0.0 7.8 %copy-start.5 = (s32[16]{0:T(128)S(1)}, s32[16]{0:T(128)}, u32[]{:S(2)}) copy-start(s32[16]{0:T(128)} %near_count.1) | copy-start | bytes 196
  0.0 18.2 %copy-start.2 = (s32[5,256]{1,0:T(8,128)S(1)}, s32[5,256]{1,0:T(8,128)}, u32[]{:S(2)}) copy-start(s32[5,256]{1,0:T(8,128)} %index.11) | copy-start | bytes 15364
  1.6 16.7 %copy-start = (bf16[5,256,512]{2,1,0:T(8,128)(2,1)S(1)}, bf16[5,256,512]{2,1,0:T(8,128)(2,1)}, u32[]{:S(2)}) copy-start(bf16[5,256,512]{2,1,0:T(8,128)(2,1)} %maps.11) | copy-start | bytes 3932164
  1.6 37.7 %collective-permute-start.4 = (bf16[96,8192]{1,0:T(8,128)(2,1)S(1)}, bf16[96,8192]{1,0:T(8,128)(2,1)}, u32[]{:S(2)}, u32[]{:S(2)}) collective-permute-start(bf16[96,8192]{1,0:T(8,128)(2,1)S(1)} %pad_maximum_fusion.both.refs_3_), channel_id=1, source_target_pairs={{0,4},{4,8},{8,12},{12,16},{16,20},{20,24},{24,28},{28,32},{32,36}... | collective-permute-start | bytes 4718600 | tf_op jit(solution)/shard_map/ppermute | solution.py:264
  5.8 42.2 %collective-permute-start.6 = (bf16[96,8192]{1,0:T(8,128)(2,1)S(1)}, bf16[96,8192]{1,0:T(8,128)(2,1)}, u32[]{:S(2)}, u32[]{:S(2)}) collective-permute-start(bf16[96,8192]{1,0:T(8,128)(2,1)S(1)} %pad_maximum_fusion.both.refs_3_), channel_id=1, source_target_pairs={{4,0},{8,4},{12,8},{16,12},{20,16},{24,20},{28,24},{32,28},{36,32}... | collective-permute-start | bytes 4718600 | tf_op jit(solution)/shard_map/ppermute | solution.py:265
  7.8 2.2 %copy-start.1 = (bf16[1,256,8192]{2,1,0:T(8,128)(2,1)S(1)}, bf16[1,256,8192]{2,1,0:T(8,128)(2,1)}, u32[]{:S(2)}) copy-start(bf16[1,256,8192]{2,1,0:T(8,128)(2,1)} %maps.6) | copy-start | bytes 12582916
  14.8 1.1 %copy-start.6 = (bf16[80,8704]{1,0:T(8,128)(2,1)}, bf16[80,8704]{1,0:T(8,128)(2,1)S(1)}, u32[]{:S(2)}) copy-start(bf16[80,8704]{1,0:T(8,128)(2,1)S(1)} %get-tuple-element.10.refs_2_.rows) | copy-start | bytes 4177924
  15.9 1.1 %copy-start.8 = (bf16[80,8192]{1,0:T(8,128)(2,1)}, bf16[80,8192]{1,0:T(8,128)(2,1)S(1)}, u32[]{:S(2)}) copy-start(bf16[80,8192]{1,0:T(8,128)(2,1)S(1)} %get-tuple-element.14.refs_4_) | copy-start | bytes 3932164
  17.0 1.2 %collective-permute-start = (bf16[96,256]{1,0:T(8,128)(2,1)S(1)}, bf16[96,256]{1,0:T(8,128)(2,1)S(1)}, u32[]{:S(2)}, u32[]{:S(2)}) collective-permute-start(bf16[96,256]{1,0:T(8,128)(2,1)S(1)} %get-tuple-element.11.own), channel_id=1, source_target_pairs={{0,4},{4,0},{8,12},{12,8},{16,20},{20,16},{24,28},{28,24},{32,36},... | collective-permute-start | bytes 147464 | tf_op jit(solution)/shard_map/ppermute | solution.py:271
  17.2 4.6 %copy-start.7 = (bf16[80,8704]{1,0:T(8,128)(2,1)S(1)}, bf16[80,8704]{1,0:T(8,128)(2,1)}, u32[]{:S(2)}) copy-start(bf16[80,8704]{1,0:T(8,128)(2,1)} %copy-done.6) | copy-start | bytes 4177924
  18.5 8.3 %collective-permute-start.1 = (bf16[96,256]{1,0:T(8,128)(2,1)S(1)}, bf16[96,256]{1,0:T(8,128)(2,1)S(1)}, u32[]{:S(2)}, u32[]{:S(2)}) collective-permute-start(bf16[96,256]{1,0:T(8,128)(2,1)S(1)} %climb.5.own), channel_id=1, source_target_pairs={{0,8},{4,12},{8,0},{12,4},{16,24},{20,28},{24,16},{28,20},{32,40},... | collective-permute-start | bytes 147464 | tf_op jit(solution)/shard_map/ppermute | solution.py:271
  21.8 1.3 %copy-start.9 = (bf16[80,8192]{1,0:T(8,128)(2,1)S(1)}, bf16[80,8192]{1,0:T(8,128)(2,1)}, u32[]{:S(2)}) copy-start(bf16[80,8192]{1,0:T(8,128)(2,1)} %copy-done.8) | copy-start | bytes 3932164
  27.2 4.8 %collective-permute-start.2 = (bf16[96,256]{1,0:T(8,128)(2,1)S(1)}, bf16[96,256]{1,0:T(8,128)(2,1)S(1)}, u32[]{:S(2)}, u32[]{:S(2)}) collective-permute-start(bf16[96,256]{1,0:T(8,128)(2,1)S(1)} %climb.6.own), channel_id=1, source_target_pairs={{0,16},{4,20},{8,24},{12,28},{16,0},{20,4},{24,8},{28,12},{32,48},... | collective-permute-start | bytes 147464 | tf_op jit(solution)/shard_map/ppermute | solution.py:271
  32.3 15.3 %collective-permute-start.3 = (bf16[96,256]{1,0:T(8,128)(2,1)S(1)}, bf16[96,256]{1,0:T(8,128)(2,1)S(1)}, u32[]{:S(2)}, u32[]{:S(2)}) collective-permute-start(bf16[96,256]{1,0:T(8,128)(2,1)S(1)} %climb.7.own), channel_id=1, source_target_pairs={{0,32},{4,36},{8,40},{12,44},{16,48},{20,52},{24,56},{28,60},{32,0... | collective-permute-start | bytes 147464 | tf_op jit(solution)/shard_map/ppermute | solution.py:271
  47.9 8.5 %collective-permute-start.5 = (bf16[96,256]{1,0:T(8,128)(2,1)S(1)}, bf16[96,256]{1,0:T(8,128)(2,1)S(1)}, u32[]{:S(2)}, u32[]{:S(2)}) collective-permute-start(bf16[96,256]{1,0:T(8,128)(2,1)S(1)} %climb.8.own), channel_id=1, source_target_pairs={{0,64},{4,68},{8,72},{12,76},{16,80},{20,84},{24,88},{28,92},{32,9... | collective-permute-start | bytes 147464 | tf_op jit(solution)/shard_map/ppermute | solution.py:271
  56.4 8.5 %copy-start.10 = (bf16[80,8192]{1,0:T(8,128)(2,1)S(1)}, bf16[80,8192]{1,0:T(8,128)(2,1)}, u32[]{:S(2)}) copy-start(bf16[80,8192]{1,0:T(8,128)(2,1)} %copy-done.8) | copy-start | bytes 3932164
  56.7 13.5 %collective-permute-start.7 = (bf16[96,256]{1,0:T(8,128)(2,1)S(1)}, bf16[96,256]{1,0:T(8,128)(2,1)S(1)}, u32[]{:S(2)}, u32[]{:S(2)}) collective-permute-start(bf16[96,256]{1,0:T(8,128)(2,1)S(1)} %climb.9), channel_id=1, source_target_pairs={{0,128},{4,132},{8,136},{12,140},{16,144},{20,148},{24,152},{28,15... | collective-permute-start | bytes 147464 | tf_op jit(solution)/shard_map/ppermute | solution.py:271
